TPU v7x, 32 devices: a whole 2x2x4 slice. The times are simulated.
32 devices in a mesh: section: 2 (over core), dp: 4 (over y, x), seq: 4 (over z).
Axes of the slice: x: 2, y: 2, z: 4, core: 2. Of those that a mesh axis runs over, the one named last changes fastest.
Arguments:
- inputs: bfloat16 [2, 16, 1024, 512], P('section', 'dp', 'seq'), may hold values from -6 to 6
- cotangent: bfloat16 [16, 1024, 512], P('dp', 'seq'), may hold values from -6 to 6
- qkv_weight: bfloat16 [2, 512, 1536], P('section'), may hold values from -0.25 to 0.25
- out_weight: bfloat16 [2, 512, 512], P('section'), may hold values from -3 to 3
- up_weight: bfloat16 [2, 512, 2048], P('section'), may hold values from -0.25 to 0.25
- down_weight: bfloat16 [2, 2048, 512], P('section'), may hold values from -0.125 to 0.125
- norm_gain: float32 [2, 2, 512], P('section'), may hold values from 0.5 to 1.5
- norm_bias: float32 [2, 2, 512], P('section'), may hold values from -1.2 to 1.2
- cross_q_weight: bfloat16 [512, 512], replicated, may hold values from -0.25 to 0.25
- cross_kv_weight: bfloat16 [512, 1024], replicated, may hold values from -0.25 to 0.25
- cross_out_weight: bfloat16 [512, 512], replicated, may hold values from -3 to 3
- cross_gain: float32 [512], replicated, may hold values from 0.5 to 1.5
- cross_bias: float32 [512], replicated, may hold values from -1.2 to 1.2
- source_segments: int32 [16, 1024], P('dp'), may hold values from 0 to 3, as said below
- target_segments: int32 [16, 1024], P('dp'), may hold values from 0 to 3, as said below
Outputs:
- layer_outputs: bfloat16 [2, 16, 1024, 512], P('section', 'dp', 'seq')
- input_grads: float32 [2, 16, 1024, 512], P('section', 'dp', 'seq')
- qkv_grad: float32 [2, 512, 1536], P('section')
- out_grad: float32 [2, 512, 512], P('section')
- up_grad: float32 [2, 512, 2048], P('section')
- down_grad: float32 [2, 2048, 512], P('section')
- gain_grad: float32 [2, 2, 512], P('section')
- bias_grad: float32 [2, 2, 512], P('section')
- cross_q_grad: float32 [512, 512], replicated
- cross_kv_grad: float32 [512, 1024], replicated
- cross_out_grad: float32 [512, 512], replicated
- cross_gain_grad: float32 [512], replicated
- cross_bias_grad: float32 [512], replicated
Inputs may be any that keep to these rules, and one draw needn't show every extreme that they name: `source_segments`: each row numbers its documents 0 to 3 in order, never falling, each document one token or more; target document j of a row is attended against source document j of the same row. `target_segments`: as for source_segments.
All inputs are finite; a program needn't handle non-finite values.
Results may differ from a plain program's by a relative error of at most 0.02.
Values may be sent and summed in bfloat16 or wider, within the bound.
A program may use at most 320 MiB of HBM per device.

v0:
```python
import jax
import jax.numpy as jnp
from jax import lax
from jax.sharding import PartitionSpec as P

DH = 64
MICRO = 2
MB_ROWS = 2


EPSILON = 1e-05
NEGATIVE = -1e30


def from_behind(value, axis, steps):
    count = lax.axis_size(axis)
    leading, last = (max(0, -steps), min(count, count - steps))
    return lax.ppermute(value, axis, [(source, source + steps) for source in range(leading, last)])


def layer_norm(vector, gain_row, bias_row):
    centre = vector - jnp.mean(vector, axis=-1, keepdims=True)
    spread = jnp.mean(centre * centre, axis=-1, keepdims=True)
    return centre * lax.rsqrt(spread + EPSILON) * gain_row + bias_row


def gelu_tanh(vector):
    return jax.nn.gelu(vector, approximate=True)


def heads_view(vector):
    return vector.reshape(vector.shape[:-1] + (vector.shape[-1] // DH, DH))


def joined_view(vector):
    return vector.reshape(vector.shape[:-2] + (vector.shape[-2] * vector.shape[-1],))


def dense_rows(left_side, right_side):
    return jnp.einsum("rsd,de->rse", left_side, right_side, preferred_element_type=jnp.float32)


def dense_back(left_side, right_side):
    return jnp.einsum("rse,de->rsd", left_side, right_side, preferred_element_type=jnp.float32)


def outer_sum(left_side, right_side):
    return jnp.einsum("rsd,rse->de", left_side, right_side, preferred_element_type=jnp.float32)


def build_mask(query_ids, key_ids, query_places, key_places, causal):
    same_doc = query_ids[:, :, None] == key_ids[:, None, :]
    ordered = (key_places[None, :] <= query_places[:, None]) | jnp.logical_not(causal)
    return same_doc & ordered[None]


def soft_forward(queries, key_rows, value_rows, allowed):
    score_scale = DH ** (-0.5)
    scores = (
        jnp.einsum(
            "rqhe,rkhe->rhqk",
            heads_view(queries),
            heads_view(key_rows),
            preferred_element_type=jnp.float32,
        )
        * score_scale
    )
    scores = jnp.where(allowed[:, None], scores, NEGATIVE)
    highest = jnp.max(scores, axis=-1, keepdims=True)
    exp_terms = jnp.exp(scores - highest)
    totals = jnp.sum(exp_terms, axis=-1, keepdims=True)
    weights = exp_terms / totals
    log_total = (highest + jnp.log(totals))[..., 0]
    mixed_out = jnp.einsum(
        "rhqk,rkhe->rqhe",
        weights.astype(jnp.bfloat16),
        heads_view(value_rows),
        preferred_element_type=jnp.float32,
    )
    return (joined_view(mixed_out), weights, log_total)


def score_grads(grad_mixed, value_rows, weights):
    grad_weights = jnp.einsum(
        "rqhe,rkhe->rhqk",
        heads_view(grad_mixed),
        heads_view(value_rows),
        preferred_element_type=jnp.float32,
    )
    inner_sum = jnp.sum(grad_weights * weights, axis=-1, keepdims=True)
    grad_scores = (weights * (grad_weights - inner_sum)).astype(jnp.bfloat16)
    return (grad_scores, inner_sum[..., 0])


def attend_keys(queries, key_rows, value_rows, query_ids, key_ids, causal):
    span_len = key_rows.shape[1]
    offset = lax.axis_index("seq") * span_len
    whole_keys, whole_values = (
        lax.all_gather(key_rows, "seq", axis=1, tiled=True),
        lax.all_gather(value_rows, "seq", axis=1, tiled=True),
    )
    own_positions = offset + jnp.arange(span_len)
    all_positions = jnp.arange(whole_keys.shape[1])
    own_ids = lax.dynamic_slice_in_dim(query_ids, offset, span_len, 1)
    allowed = build_mask(own_ids, key_ids, own_positions, all_positions, causal)
    mixed_out, weights, log_total = soft_forward(queries, whole_keys, whole_values, allowed)
    kept_state = (
        queries,
        key_rows,
        value_rows,
        whole_keys,
        whole_values,
        weights,
        log_total,
        query_ids,
        key_ids,
        causal,
    )
    return (mixed_out, kept_state)


def attend_back(kept_state, grad_mixed):
    (
        queries,
        key_rows,
        value_rows,
        whole_keys,
        whole_values,
        weights,
        log_total,
        query_ids,
        key_ids,
        causal,
    ) = kept_state
    score_scale = DH ** (-0.5)
    grad_scores, inner_sum = score_grads(grad_mixed, whole_values, weights)
    grad_queries = (
        jnp.einsum(
            "rhqk,rkhe->rqhe",
            grad_scores,
            heads_view(whole_keys),
            preferred_element_type=jnp.float32,
        )
        * score_scale
    )
    part_keys = (
        jnp.einsum(
            "rhqk,rqhe->rkhe", grad_scores, heads_view(queries), preferred_element_type=jnp.float32
        )
        * score_scale
    )
    part_values = jnp.einsum(
        "rhqk,rqhe->rkhe",
        weights.astype(jnp.bfloat16),
        heads_view(grad_mixed),
        preferred_element_type=jnp.float32,
    )
    grad_keys, grad_values = (
        lax.psum_scatter(
            joined_view(part_keys).astype(jnp.bfloat16), "seq", scatter_dimension=1, tiled=True
        ).astype(jnp.float32),
        lax.psum_scatter(
            joined_view(part_values).astype(jnp.bfloat16), "seq", scatter_dimension=1, tiled=True
        ).astype(jnp.float32),
    )
    return (joined_view(grad_queries), grad_keys, grad_values)


def layer_forward(tokens, memory_in, own_ids, source_ids, target_ids, params, decoder):
    (
        qkv_matrix,
        out_matrix,
        up_matrix,
        down_matrix,
        norm_gains,
        norm_biases,
        query_matrix,
        pair_matrix,
        cross_matrix,
        cross_gains,
        cross_shift,
    ) = params
    residual = tokens.astype(jnp.float32)
    packed = dense_rows(tokens, qkv_matrix).astype(jnp.bfloat16)
    queries, key_rows, value_rows = jnp.split(packed, 3, axis=-1)
    mixed_out, self_state = attend_keys(queries, key_rows, value_rows, own_ids, own_ids, decoder)
    mixed_low = mixed_out.astype(jnp.bfloat16)
    first_sum = residual + dense_rows(mixed_low, out_matrix)
    first_norm = layer_norm(first_sum, norm_gains[0], norm_biases[0])
    first_low = first_norm.astype(jnp.bfloat16)
    cross_query = dense_rows(first_low, query_matrix).astype(jnp.bfloat16)
    cross_pair = dense_rows(memory_in, pair_matrix).astype(jnp.bfloat16)
    cross_keys, cross_values = jnp.split(cross_pair, 2, axis=-1)
    cross_mixed, cross_state = attend_keys(
        cross_query, cross_keys, cross_values, target_ids, source_ids, False
    )
    cross_low = cross_mixed.astype(jnp.bfloat16)
    cross_sum = first_norm + dense_rows(cross_low, cross_matrix)
    second = jnp.where(decoder, layer_norm(cross_sum, cross_gains, cross_shift), first_norm)
    second_low = second.astype(jnp.bfloat16)
    upward = dense_rows(second_low, up_matrix)
    gated_low = gelu_tanh(upward).astype(jnp.bfloat16)
    last_sum = second + dense_rows(gated_low, down_matrix)
    output = layer_norm(last_sum, norm_gains[1], norm_biases[1])
    kept_state = (
        tokens,
        self_state,
        mixed_low,
        first_sum,
        first_low,
        cross_state,
        cross_low,
        cross_sum,
        second_low,
        upward,
        gated_low,
        last_sum,
    )
    return (output, kept_state)


def layer_backward(kept_state, grad_out, params, decoder):
    (
        qkv_matrix,
        out_matrix,
        up_matrix,
        down_matrix,
        norm_gains,
        norm_biases,
        query_matrix,
        pair_matrix,
        cross_matrix,
        cross_gains,
        cross_shift,
    ) = params
    (
        tokens,
        self_state,
        mixed_low,
        first_sum,
        first_low,
        cross_state,
        cross_low,
        cross_sum,
        second_low,
        upward,
        gated_low,
        last_sum,
    ) = kept_state
    unused, pull_last = jax.vjp(layer_norm, last_sum, norm_gains[1], norm_biases[1])
    grad_last, grad_gain_last, grad_bias_last = pull_last(grad_out)
    down_in = grad_last.astype(jnp.bfloat16)
    grad_down = outer_sum(gated_low, down_in)
    grad_gated = dense_back(down_in, down_matrix)
    unused, pull_gelu = jax.vjp(gelu_tanh, upward)
    up_in = pull_gelu(grad_gated)[0].astype(jnp.bfloat16)
    grad_up = outer_sum(second_low, up_in)
    grad_second = grad_last + dense_back(up_in, up_matrix)
    unused, pull_cross = jax.vjp(layer_norm, cross_sum, cross_gains, cross_shift)
    grad_cross_sum, grad_cross_gain, grad_cross_bias = pull_cross(
        jnp.where(decoder, grad_second, 0.0)
    )
    grad_first = jnp.where(decoder, grad_cross_sum, grad_second)
    cross_in = grad_cross_sum.astype(jnp.bfloat16)
    grad_cross_out = outer_sum(cross_low, cross_in)
    grad_cross_mixed = dense_back(cross_in, cross_matrix).astype(jnp.bfloat16)
    grad_cross_query, grad_cross_keys, grad_cross_values = attend_back(
        cross_state, grad_cross_mixed
    )
    query_in = grad_cross_query.astype(jnp.bfloat16)
    grad_query_matrix = outer_sum(first_low, query_in)
    grad_first = grad_first + dense_back(query_in, query_matrix)
    pair_in = jnp.concatenate([grad_cross_keys, grad_cross_values], axis=-1).astype(jnp.bfloat16)
    unused, pull_first = jax.vjp(layer_norm, first_sum, norm_gains[0], norm_biases[0])
    grad_first_sum, grad_gain_first, grad_bias_first = pull_first(grad_first)
    out_in = grad_first_sum.astype(jnp.bfloat16)
    grad_out_matrix = outer_sum(mixed_low, out_in)
    grad_mixed = dense_back(out_in, out_matrix).astype(jnp.bfloat16)
    grad_queries, grad_keys, grad_values = attend_back(self_state, grad_mixed)
    qkv_in = jnp.concatenate([grad_queries, grad_keys, grad_values], axis=-1).astype(jnp.bfloat16)
    grad_qkv_matrix = outer_sum(tokens, qkv_in)
    grad_tokens = grad_first_sum + dense_back(qkv_in, qkv_matrix)
    grad_set = (
        grad_qkv_matrix,
        grad_out_matrix,
        grad_up,
        grad_down,
        jnp.stack([grad_gain_first, grad_gain_last]),
        jnp.stack([grad_bias_first, grad_bias_last]),
        grad_query_matrix,
        jnp.zeros(pair_matrix.shape, jnp.float32),
        grad_cross_out,
        grad_cross_gain,
        grad_cross_bias,
    )
    return (grad_tokens, pair_in, grad_set)


def shards(
    inputs,
    cotangent,
    qkv_weight,
    out_weight,
    up_weight,
    down_weight,
    norm_gain,
    norm_bias,
    cross_q_weight,
    cross_kv_weight,
    cross_out_weight,
    cross_gain,
    cross_bias,
    source_segments,
    target_segments,
):
    section_index = lax.axis_index("section")
    decoder = section_index == 1
    params = (
        qkv_weight[0],
        out_weight[0],
        up_weight[0],
        down_weight[0],
        norm_gain[0],
        norm_bias[0],
        cross_q_weight,
        cross_kv_weight,
        cross_out_weight,
        cross_gain,
        cross_bias,
    )
    tokens_all = inputs[0]
    own_all = jnp.where(decoder, target_segments, source_segments)
    span_len = tokens_all.shape[1]
    features = tokens_all.shape[2]
    memory_in = jnp.zeros((MB_ROWS, span_len, features), jnp.bfloat16)
    outputs_all = jnp.zeros(tokens_all.shape, jnp.bfloat16)
    caches = []
    sent_rows = []
    for forward_tick in range(MICRO + 1):
        micro_index = forward_tick - section_index
        active = (micro_index >= 0) & (micro_index < MICRO)
        first_row = jnp.clip(micro_index, 0, MICRO - 1) * MB_ROWS
        rows_now = lax.dynamic_slice_in_dim(tokens_all, first_row, MB_ROWS, 0)
        own_now = lax.dynamic_slice_in_dim(own_all, first_row, MB_ROWS, 0)
        source_now = lax.dynamic_slice_in_dim(source_segments, first_row, MB_ROWS, 0)
        target_now = lax.dynamic_slice_in_dim(target_segments, first_row, MB_ROWS, 0)
        output, kept_state = layer_forward(
            rows_now, memory_in, own_now, source_now, target_now, params, decoder
        )
        output_low = output.astype(jnp.bfloat16)
        current = lax.dynamic_slice_in_dim(outputs_all, first_row, MB_ROWS, 0)
        outputs_all = lax.dynamic_update_slice_in_dim(
            outputs_all, jnp.where(active, output_low, current), first_row, 0
        )
        caches.append(kept_state)
        sent_rows.append(output_low)
        if forward_tick < MICRO:
            memory_in = from_behind(output_low, "section", 1)
    grad_pair_in = jnp.zeros((MB_ROWS, span_len, 2 * features), jnp.bfloat16)
    totals = tuple((jnp.zeros(param_item.shape, jnp.float32) for param_item in params))
    input_all = jnp.zeros(tokens_all.shape, jnp.float32)
    for backward_tick in range(MICRO + 1):
        forward_tick = MICRO - backward_tick
        micro_index = forward_tick - section_index
        active = (micro_index >= 0) & (micro_index < MICRO)
        first_row = jnp.clip(micro_index, 0, MICRO - 1) * MB_ROWS
        cot_now = lax.dynamic_slice_in_dim(cotangent, first_row, MB_ROWS, 0).astype(jnp.float32)
        memory_grad = lax.optimization_barrier(
            dense_back(grad_pair_in, params[7]).astype(jnp.bfloat16)
        ).astype(jnp.float32)
        pair_term = outer_sum(sent_rows[forward_tick], grad_pair_in)
        grad_out = jnp.where(decoder, cot_now, memory_grad)
        grad_tokens, pair_in, grad_set = layer_backward(
            caches[forward_tick], grad_out, params, decoder
        )
        grad_set = grad_set[:7] + (jnp.where(decoder, 0.0, pair_term),) + grad_set[8:]
        totals = jax.tree.map(
            lambda total_sum, new_term: total_sum + jnp.where(active, new_term, 0.0),
            totals,
            grad_set,
        )
        current = lax.dynamic_slice_in_dim(input_all, first_row, MB_ROWS, 0)
        input_all = lax.dynamic_update_slice_in_dim(
            input_all, jnp.where(active, grad_tokens, current), first_row, 0
        )
        if backward_tick < MICRO:
            grad_pair_in = from_behind(pair_in, "section", -1)
    layer_part = lax.psum(
        (totals[0], totals[1], totals[2], totals[3], totals[4], totals[5]), ("dp", "seq")
    )
    cross_part = lax.psum(
        (totals[6], totals[7], totals[8], totals[9], totals[10]), ("section", "dp", "seq")
    )
    return (
        outputs_all[None],
        input_all[None],
        layer_part[0][None],
        layer_part[1][None],
        layer_part[2][None],
        layer_part[3][None],
        layer_part[4][None],
        layer_part[5][None],
        cross_part[0],
        cross_part[1],
        cross_part[2],
        cross_part[3],
        cross_part[4],
    )


def solution(mesh):
    in_specs = (
        P("section", "dp", "seq", None),
        P("dp", "seq", None),
        P("section", None, None),
        P("section", None, None),
        P("section", None, None),
        P("section", None, None),
        P("section", None, None),
        P("section", None, None),
        P(),
        P(),
        P(),
        P(),
        P(),
        P("dp", None),
        P("dp", None),
    )
    out_specs = (
        P("section", "dp", "seq", None),
        P("section", "dp", "seq", None),
        P("section", None, None),
        P("section", None, None),
        P("section", None, None),
        P("section", None, None),
        P("section", None, None),
        P("section", None, None),
        P(),
        P(),
        P(),
        P(),
        P(),
    )
    return jax.shard_map(shards, mesh=mesh, in_specs=in_specs, out_specs=out_specs, check_vma=False)
```

profile of v0, /device:TPU:1, one launch (start us, length us, event | category | flops | bytes accessed | tf_op | source)
XLA Modules:
  0.0 1756.8 jit_solution(13260141469720208249)
XLA Ops:
  24.1 35.2 %all-gather.15.cloned.1.call-done = bf16[2,1024,512]{2,1,0:T(8,128)(2,1)} async-done(((bf16[2,256,512]{2,1,0:T(8,128)(2,1)}), bf16[2,1024,512]{2,1,0:T(8,128)(2,1)}) %all-gather.15.cloned.1.call-update) | async-done | bytes 2097168 | tf_op jit(solution)/shard_map/all_gather | solution.py:99
  73.9 32.2 %all-gather.13.cloned.1.call-done = bf16[2,1024,512]{2,1,0:T(8,128)(2,1)} async-done(((bf16[2,256,512]{2,1,0:T(8,128)(2,1)}), bf16[2,1024,512]{2,1,0:T(8,128)(2,1)}) %all-gather.13.cloned.1.call-update) | async-done | bytes 2097168 | tf_op jit(solution)/shard_map/all_gather | solution.py:100
  124.3 28.6 %all-gather.19.cloned.1.call-done = bf16[2,1024,512]{2,1,0:T(8,128)(2,1)} async-done(((bf16[2,256,512]{2,1,0:T(8,128)(2,1)}), bf16[2,1024,512]{2,1,0:T(8,128)(2,1)}) %all-gather.19.cloned.1.call-update) | async-done | bytes 2097168 | tf_op jit(solution)/shard_map/all_gather | solution.py:99
  167.7 31.8 %all-gather.17.cloned.1.call-done = bf16[2,1024,512]{2,1,0:T(8,128)(2,1)} async-done(((bf16[2,256,512]{2,1,0:T(8,128)(2,1)}), bf16[2,1024,512]{2,1,0:T(8,128)(2,1)}) %all-gather.17.cloned.1.call-update) | async-done | bytes 2097168 | tf_op jit(solution)/shard_map/all_gather | solution.py:100
  234.1 11.6 all-gather.23.cloned.1.call-done
  260.7 31.0 %all-gather.21.cloned.1.call-done = bf16[2,1024,512]{2,1,0:T(8,128)(2,1)} async-done(((bf16[2,256,512]{2,1,0:T(8,128)(2,1)}), bf16[2,1024,512]{2,1,0:T(8,128)(2,1)}) %all-gather.21.cloned.1.call-update) | async-done | bytes 2097168 | tf_op jit(solution)/shard_map/all_gather | solution.py:100
  310.1 28.5 %all-gather.27.cloned.1.call-done = bf16[2,1024,512]{2,1,0:T(8,128)(2,1)} async-done(((bf16[2,256,512]{2,1,0:T(8,128)(2,1)}), bf16[2,1024,512]{2,1,0:T(8,128)(2,1)}) %all-gather.27.cloned.1.call-update) | async-done | bytes 2097168 | tf_op jit(solution)/shard_map/all_gather | solution.py:99
  353.5 31.9 %all-gather.25.cloned.1.call-done = bf16[2,1024,512]{2,1,0:T(8,128)(2,1)} async-done(((bf16[2,256,512]{2,1,0:T(8,128)(2,1)}), bf16[2,1024,512]{2,1,0:T(8,128)(2,1)}) %all-gather.25.cloned.1.call-update) | async-done | bytes 2097168 | tf_op jit(solution)/shard_map/all_gather | solution.py:100
  418.8 12.9 all-gather.31.cloned.1.call-done
  435.7 42.1 %all-gather.29.cloned.1.call-done = bf16[2,1024,512]{2,1,0:T(8,128)(2,1)} async-done(((bf16[2,256,512]{2,1,0:T(8,128)(2,1)}), bf16[2,1024,512]{2,1,0:T(8,128)(2,1)}) %all-gather.29.cloned.1.call-update) | async-done | bytes 2097168 | tf_op jit(solution)/shard_map/all_gather | solution.py:100
  506.8 17.9 %all-gather.35.cloned.1.call-done = bf16[2,1024,512]{2,1,0:T(8,128)(2,1)} async-done(((bf16[2,256,512]{2,1,0:T(8,128)(2,1)}), bf16[2,1024,512]{2,1,0:T(8,128)(2,1)}) %all-gather.35.cloned.1.call-update) | async-done | bytes 2097168 | tf_op jit(solution)/shard_map/all_gather | solution.py:99
  539.5 31.2 %all-gather.33.cloned.1.call-done = bf16[2,1024,512]{2,1,0:T(8,128)(2,1)} async-done(((bf16[2,256,512]{2,1,0:T(8,128)(2,1)}), bf16[2,1024,512]{2,1,0:T(8,128)(2,1)}) %all-gather.33.cloned.1.call-update) | async-done | bytes 2097168 | tf_op jit(solution)/shard_map/all_gather | solution.py:100
  600.0 11.4 multiply_reduce_fusion.5
  611.4 11.6 multiply_convert_fusion.5
  643.3 30.3 %reduce-scatter.15.cloned.1.call-done = bf16[2,256,512]{2,1,0:T(8,128)(2,1)} async-done(((bf16[2,1024,512]{2,1,0:T(8,128)(2,1)}), bf16[2,256,512]{2,1,0:T(8,128)(2,1)}) %reduce-scatter.15.cloned.1.call-update) | async-done | bytes 524304 | tf_op jit(solution)/shard_map/reduce_scatter | solution.py:159
  673.6 45.5 %reduce-scatter.17.cloned.1.call-done = bf16[2,256,512]{2,1,0:T(8,128)(2,1)} async-done(((bf16[2,1024,512]{2,1,0:T(8,128)(2,1)}), bf16[2,256,512]{2,1,0:T(8,128)(2,1)}) %reduce-scatter.17.cloned.1.call-update) | async-done | bytes 524304 | tf_op jit(solution)/shard_map/reduce_scatter | solution.py:162
  750.6 11.6 multiply_convert_fusion.3
  790.1 22.8 %reduce-scatter.23.cloned.1.call-done = bf16[2,256,512]{2,1,0:T(8,128)(2,1)} async-done(((bf16[2,1024,512]{2,1,0:T(8,128)(2,1)}), bf16[2,256,512]{2,1,0:T(8,128)(2,1)}) %reduce-scatter.23.cloned.1.call-update) | async-done | bytes 524304 | tf_op jit(solution)/shard_map/reduce_scatter | solution.py:159
  812.9 45.5 %reduce-scatter.25.cloned.1.call-done = bf16[2,256,512]{2,1,0:T(8,128)(2,1)} async-done(((bf16[2,1024,512]{2,1,0:T(8,128)(2,1)}), bf16[2,256,512]{2,1,0:T(8,128)(2,1)}) %reduce-scatter.25.cloned.1.call-update) | async-done | bytes 524304 | tf_op jit(solution)/shard_map/reduce_scatter | solution.py:162
  895.6 14.3 fusion.237
  917.7 11.5 multiply_reduce_fusion.2
  929.3 11.7 multiply_convert_fusion.2
  961.5 11.6 multiply_reduce_fusion.4
  973.1 11.7 multiply_convert_fusion.4
  1015.9 11.6 multiply_reduce_fusion
  1027.5 11.7 multiply_convert_fusion
  1135.4 36.2 %reduce-scatter.27.cloned.1.call-done = bf16[2,256,512]{2,1,0:T(8,128)(2,1)} async-done(((bf16[2,1024,512]{2,1,0:T(8,128)(2,1)}), bf16[2,256,512]{2,1,0:T(8,128)(2,1)}) %reduce-scatter.27.cloned.1.call-update) | async-done | bytes 524304 | tf_op jit(solution)/shard_map/reduce_scatter | solution.py:159
  1171.6 46.2 %reduce-scatter.29.cloned.1.call-done = bf16[2,256,512]{2,1,0:T(8,128)(2,1)} async-done(((bf16[2,1024,512]{2,1,0:T(8,128)(2,1)}), bf16[2,256,512]{2,1,0:T(8,128)(2,1)}) %reduce-scatter.29.cloned.1.call-update) | async-done | bytes 524304 | tf_op jit(solution)/shard_map/reduce_scatter | solution.py:162
  1226.6 40.1 %all-reduce = (f32[512]{0:T(512)}, f32[512]{0:T(512)}) all-reduce(f32[512]{0:T(512)S(1)} %select_add_fusion.1, f32[512]{0:T(512)S(1)} %select_add_fusion), channel_id=1, replica_groups=mesh['section'=2,'dp'=4,'seq'=4] {'section','dp','seq'}, use_global_device_ids=true, to_apply=%region_88.89 | all-reduce | flops 1024 | bytes 8192 | tf_op jit(solution)/shard_map/psum | solution.py:391
  1266.9 34.5 %all-reduce.2 = (f32[1,2,512]{2,1,0:T(2,128)}, f32[1,2,512]{2,1,0:T(2,128)}) all-reduce(f32[1,2,512]{2,1,0:T(2,128)S(1)} %fusion.309, f32[1,2,512]{2,1,0:T(2,128)S(1)} %fusion.312), channel_id=1, replica_groups=mesh['section'=2,'dp'=4,'seq'=4] {'dp','seq'}, use_global_device_ids=true, to_apply=%region_74.75 | all-reduce | flops 2048 | bytes 16384 | tf_op jit(solution)/shard_map/psum | solution.py:388
  1310.0 55.6 %all-reduce.7.cloned.1.call-done = (f32[512,512]{1,0:T(8,128)}, f32[512,1024]{1,0:T(8,128)}, f32[512,512]{1,0:T(8,128)}) async-done(((f32[512,512]{1,0:T(8,128)}, f32[512,1024]{1,0:T(8,128)}, f32[512,512]{1,0:T(8,128)}), (f32[512,512]{1,0:T(8,128)}, f32[512,1024]{1,0:T(8,128)}, f32[512,512]{1,0:T(8,128)})) %all-reduce.7.cloned.1.call-update) | async-done | bytes 4194320 | tf_op jit(solution)/shard_map/psum | solution.py:391
  1365.6 369.5 %all-reduce.9.cloned.1.call-done = (f32[1,512,1536]{2,1,0:T(8,128)}, f32[1,512,512]{2,1,0:T(8,128)}, f32[1,512,2048]{2,1,0:T(8,128)}, f32[1,2048,512]{2,1,0:T(8,128)}) async-done(((f32[1,512,1536]{2,1,0:T(8,128)}, f32[1,512,512]{2,1,0:T(8,128)}, f32[1,512,2048]{2,1,0:T(8,128)}, f32[1,2048,512]{2,1,0:T(8,128)}), (f32[1,512,1536]{2,1,0:T(8,128)}, f32[1,512,512]{2,1,0:T(8,128)}, f32[1,512,2048]{2,1,0:T(8,128)}, ...) | async-done | bytes 12582928 | tf_op jit(solution)/shard_map/psum | solution.py:388
  (833 shorter events, 559.2 us)
Async XLA Ops:
  7.2 52.1 %all-gather.15.cloned.1.call-start = ((), (), s32[]{:S(2)}) async-start(), calls=%async_computation.11 | async-start | bytes 2621440 | tf_op jit(solution)/shard_map/all_gather | solution.py:99
  11.1 94.9 %all-gather.13.cloned.1.call-start = ((), (), s32[]{:S(2)}) async-start(), calls=%async_computation.10 | async-start | bytes 2621440 | tf_op jit(solution)/shard_map/all_gather | solution.py:100
  11.9 141.0 %all-gather.19.cloned.1.call-start = ((), (), s32[]{:S(2)}) async-start(), calls=%async_computation.13 | async-start | bytes 2621440 | tf_op jit(solution)/shard_map/all_gather | solution.py:99
  15.0 184.6 %all-gather.17.cloned.1.call-start = ((), (), s32[]{:S(2)}) async-start(), calls=%async_computation.12 | async-start | bytes 2621440 | tf_op jit(solution)/shard_map/all_gather | solution.py:100
  15.6 230.1 %all-gather.23.cloned.1.call-start = ((), (), s32[]{:S(2)}) async-start(), calls=%async_computation.15 | async-start | bytes 2621440 | tf_op jit(solution)/shard_map/all_gather | solution.py:99
  19.3 272.5 %all-gather.21.cloned.1.call-start = ((), (), s32[]{:S(2)}) async-start(), calls=%async_computation.14 | async-start | bytes 2621440 | tf_op jit(solution)/shard_map/all_gather | solution.py:100
  19.9 318.7 %all-gather.27.cloned.1.call-start = ((), (), s32[]{:S(2)}) async-start(), calls=%async_computation.17 | async-start | bytes 2621440 | tf_op jit(solution)/shard_map/all_gather | solution.py:99
  20.1 564.8 %copy-start.150 = (f32[1,1,512]{2,1,0:T(1,128)}, f32[1,1,512]{2,1,0:T(1,128)S(1)}, u32[]{:S(2)}) copy-start(f32[1,1,512]{2,1,0:T(1,128)S(1)} %get-tuple-element.103) | copy-start | bytes 6148
  20.1 385.5 %copy-start.178 = (f32[1,1,512]{2,1,0:T(1,128)}, f32[1,1,512]{2,1,0:T(1,128)S(1)}, u32[]{:S(2)}) copy-start(f32[1,1,512]{2,1,0:T(1,128)S(1)} %get-tuple-element.106) | copy-start | bytes 6148
  20.1 564.7 %copy-start.156 = (f32[1,1,512]{2,1,0:T(1,128)}, f32[1,1,512]{2,1,0:T(1,128)S(1)}, u32[]{:S(2)}) copy-start(f32[1,1,512]{2,1,0:T(1,128)S(1)} %get-tuple-element.105) | copy-start | bytes 6148
  221.9 3.8 collective-permute-start
  227.6 157.9 %all-gather.25.cloned.1.call-start = ((), (), s32[]{:S(2)}) async-start(), calls=%async_computation.16 | async-start | bytes 2621440 | tf_op jit(solution)/shard_map/all_gather | solution.py:100
  228.3 203.4 %all-gather.31.cloned.1.call-start = ((), (), s32[]{:S(2)}) async-start(), calls=%async_computation.19 | async-start | bytes 2621440 | tf_op jit(solution)/shard_map/all_gather | solution.py:99
  232.0 245.8 %all-gather.29.cloned.1.call-start = ((), (), s32[]{:S(2)}) async-start(), calls=%async_computation.18 | async-start | bytes 2621440 | tf_op jit(solution)/shard_map/all_gather | solution.py:100
  232.6 292.1 %all-gather.35.cloned.1.call-start = ((), (), s32[]{:S(2)}) async-start(), calls=%async_computation.21 | async-start | bytes 2621440 | tf_op jit(solution)/shard_map/all_gather | solution.py:99
  408.8 3.8 collective-permute-start.1
  414.4 156.4 %all-gather.33.cloned.1.call-start = ((), (), s32[]{:S(2)}) async-start(), calls=%async_computation.20 | async-start | bytes 2621440 | tf_op jit(solution)/shard_map/all_gather | solution.py:100
  492.5 181.1 %reduce-scatter.15.cloned.1.call-start = ((), (), s32[]{:S(2)}) async-start(), calls=%async_computation.24 | async-start | bytes 2621440 | tf_op jit(solution)/shard_map/reduce_scatter | solution.py:159
  598.3 264.4 %copy-start.170 = (f32[2,256]{1,0:T(2,128)}, f32[2,256]{1,0:T(2,128)S(1)}, u32[]{:S(2)}) copy-start(f32[2,256]{1,0:T(2,128)S(1)} %negate_multiply_fusion.7) | copy-start | bytes 6148
  630.8 88.3 %reduce-scatter.17.cloned.1.call-start = ((), (), s32[]{:S(2)}) async-start(), calls=%async_computation.25 | async-start | bytes 2621440 | tf_op jit(solution)/shard_map/reduce_scatter | solution.py:162
  643.3 169.7 %reduce-scatter.23.cloned.1.call-start = ((), (), s32[]{:S(2)}) async-start(), calls=%async_computation.28 | async-start | bytes 2621440 | tf_op jit(solution)/shard_map/reduce_scatter | solution.py:159
  720.5 5.3 collective-permute-start.2
  770.0 88.4 %reduce-scatter.25.cloned.1.call-start = ((), (), s32[]{:S(2)}) async-start(), calls=%async_computation.29 | async-start | bytes 2621440 | tf_op jit(solution)/shard_map/reduce_scatter | solution.py:162
  782.5 344.0 %reduce-scatter.19.cloned.1.call-start = ((), (), s32[]{:S(2)}) async-start(), calls=%async_computation.26 | async-start | bytes 2621440 | tf_op jit(solution)/shard_map/reduce_scatter | solution.py:159
  859.9 13.3 collective-permute-start.3
  947.0 179.5 %reduce-scatter.21.cloned.1.call-start = ((), (), s32[]{:S(2)}) async-start(), calls=%async_computation.27 | async-start | bytes 2621440 | tf_op jit(solution)/shard_map/reduce_scatter | solution.py:162
  961.5 169.0 %reduce-scatter.11.cloned.1.call-start = ((), (), s32[]{:S(2)}) async-start(), calls=%async_computation.22 | async-start | bytes 2621440 | tf_op jit(solution)/shard_map/reduce_scatter | solution.py:159
  992.9 137.6 %reduce-scatter.13.cloned.1.call-start = ((), (), s32[]{:S(2)}) async-start(), calls=%async_computation.23 | async-start | bytes 2621440 | tf_op jit(solution)/shard_map/reduce_scatter | solution.py:162
  1015.9 155.8 %reduce-scatter.27.cloned.1.call-start = ((), (), s32[]{:S(2)}) async-start(), calls=%async_computation.30 | async-start | bytes 2621440 | tf_op jit(solution)/shard_map/reduce_scatter | solution.py:159
  1047.4 170.4 %reduce-scatter.29.cloned.1.call-start = ((), (), s32[]{:S(2)}) async-start(), calls=%async_computation.31 | async-start | bytes 2621440 | tf_op jit(solution)/shard_map/reduce_scatter | solution.py:162
  1073.5 292.1 %all-reduce.7.cloned.1.call-start = ((), (), s32[]{:S(2)}) async-start(), calls=%async_computation.32 | async-start | bytes 8388608 | tf_op jit(solution)/shard_map/psum | solution.py:391
  1108.0 627.1 %all-reduce.9.cloned.1.call-start = ((), (), s32[]{:S(2)}) async-start(), calls=%async_computation.33 | async-start | bytes 25165824 | tf_op jit(solution)/shard_map/psum | solution.py:388
  (269 other events, 3667.4 us)
Sparse Core Ops, SparseCore 0:
  11.3 47.9 all-gather.14
  61.4 44.6 all-gather.12
  108.2 44.6 all-gather.18
  154.9 44.6 all-gather.16
  201.0 44.6 all-gather.22
  247.1 44.6 all-gather.20
  293.9 44.6 all-gather.26
  340.8 44.6 all-gather.24
  387.0 44.6 all-gather.30
  433.1 44.6 all-gather.28
  480.0 44.6 all-gather.34
  526.1 44.5 all-gather.32
  630.9 42.6 reduce-scatter.14
  675.8 43.1 reduce-scatter.16
  770.2 42.7 reduce-scatter.22
  815.2 43.1 reduce-scatter.24
  947.1 42.5 reduce-scatter.18
  992.0 43.1 reduce-scatter.20
  1037.4 43.1 reduce-scatter.10
  1082.9 43.1 reduce-scatter.12
  1128.4 43.1 reduce-scatter.26
  1174.6 43.1 reduce-scatter.28
  1224.2 141.3 all-reduce.6
  1372.4 362.5 all-reduce.8
where the time goes:
time: 1760 us
  waiting for transfers between devices  997 us (57%)
  matrix products  424 us (24%)
  local copies, waits for them, and re-layouts  149 us (8%)
  other arithmetic  83.9 us (5%)
  blocking collectives  74.6 us (4%)
  between operations  17.8 us (1%)
    psum x1, waiting for transfers between devices, shards(): lax.psum((totals[0], totals[1], totals[2], totals[3], totals[4], totals[5...  369 us
    all_gather x6, waiting for transfers between devices, attend_keys(): lax.all_gather(value_rows, 'seq', axis=1, tiled=True)  200 us
    reduce_scatter x5, waiting for transfers between devices, attend_back(): lax.psum_scatter(joined_view(part_values).astype(jnp.bfloat16), 'seq', sc...  137 us
    all_gather x6, waiting for transfers between devices, attend_keys(): lax.all_gather(key_rows, 'seq', axis=1, tiled=True)  135 us
    reduce_scatter x5, waiting for transfers between devices, attend_back(): lax.psum_scatter(joined_view(part_keys).astype(jnp.bfloat16), 'seq', scat...  89.3 us
    dot_general x21, matrix products, outer_sum(): jnp.einsum('rsd,rse->de', left_side, right_side, preferred_element_type=j...  71.6 us
    dot_general x6, matrix products, score_grads(): jnp.einsum('rqhe,rkhe->rhqk', heads_view(grad_mixed), heads_view(value_ro...  68.7 us
    sub x6, matrix products, soft_forward(): exp_terms = jnp.exp(scores - highest)  64.8 us
  transfers between devices with their start and end apart: 28, of which 23 were waited for; matrix products, arithmetic and copies ran while one was open for 25% of the time, Pallas kernels for 0%

commit v1 on v0

--- a/solution.py
+++ b/solution.py
@@ -1,6 +1,10 @@
+import functools
+
 import jax
 import jax.numpy as jnp
 from jax import lax
+from jax.experimental import pallas as pl
+from jax.experimental.pallas import tpu as pltpu
 from jax.sharding import PartitionSpec as P
 
 DH = 64
@@ -408,6 +412,576 @@
     )
 
 
+BF = jnp.bfloat16
+F32 = jnp.float32
+AXES = ("section", "dp", "seq")
+PAIR = 2 * DH
+STAT = 8
+
+
+def swap(value, move):
+    pairs = []
+    for core in range(2):
+        for group in range(4):
+            for depth in range(4):
+                to = move(core, group, depth)
+                if to is not None:
+                    pairs.append(
+                        ((core * 4 + group) * 4 + depth, (to[0] * 4 + to[1]) * 4 + to[2])
+                    )
+    return lax.ppermute(value, AXES, pairs)
+
+
+def to_core(value):
+    return swap(value, lambda core, group, depth: (1 - core, group, depth))
+
+
+def side_of(depth):
+    return (depth ^ (depth >> 1)) & 1
+
+
+def block_of(core, at):
+    return 2 * at + (core ^ at)
+
+
+def pick(parts, order):
+    odd = (order & 1) == 1
+    high = (order & 2) == 2
+    a = [jnp.where(odd, parts[j ^ 1], parts[j]) for j in range(4)]
+    return [jnp.where(high, a[j ^ 2], a[j]) for j in range(4)]
+
+
+def replace_block(whole, block, at, axis):
+    size, count = block.shape[axis], whole.shape[axis]
+    parts = [lax.slice_in_dim(whole, 0, at, axis=axis)] if at > 0 else []
+    parts.append(block)
+    if at + size < count:
+        parts.append(lax.slice_in_dim(whole, at + size, count, axis=axis))
+    return jnp.concatenate(parts, axis=axis)
+
+
+def attend_kernel(causal, q_ref, k_ref, v_ref, ko_ref, vo_ref, qf_ref, kf_ref, kfo_ref, o_ref, lse_ref):
+    size = q_ref.shape[0]
+    half = size // 2
+    lane = lax.broadcasted_iota(jnp.int32, (size, PAIR), 1)
+    low_lanes = lane < DH
+    q = q_ref[...] * jnp.array(DH ** (-0.5), BF)
+    qf, kf, kfo = qf_ref[...], kf_ref[...], kfo_ref[...]
+    k, v, ko, vo = k_ref[...], v_ref[...], ko_ref[...], vo_ref[...]
+    one = jnp.ones_like(v)
+    outs, stats = [], []
+    for head in range(2):
+        mine = low_lanes if head == 0 else jnp.logical_not(low_lanes)
+        qa = jnp.where(mine, q, qf)
+        ka = jnp.concatenate([jnp.where(mine, k, kf), jnp.where(mine, ko, kfo)], axis=0)
+        va = jnp.concatenate([jnp.where(mine, v, one), jnp.where(mine, vo, one)], axis=0)
+        if causal:
+            pieces = [
+                (0, half, [(0, half), (size, size + half)], 0),
+                (half, size, [(0, 2 * size)], half),
+            ]
+        else:
+            pieces = [(0, size, [(0, 2 * size)], None)]
+        o_rows, s_rows = [], []
+        for start, stop, spans, diagonal in pieces:
+            kk = jnp.concatenate([ka[a:b] for a, b in spans], axis=0)
+            vv = jnp.concatenate([va[a:b] for a, b in spans], axis=0)
+            s = lax.dot_general(
+                qa[start:stop], kk, (((1,), (1,)), ((), ())), preferred_element_type=F32
+            )
+            if diagonal is not None:
+                row = lax.broadcasted_iota(jnp.int32, (half, half), 0)
+                col = lax.broadcasted_iota(jnp.int32, (half, half), 1)
+                cut = jnp.where(col <= row, s[:, diagonal : diagonal + half], NEGATIVE)
+                s = replace_block(s, cut, diagonal, 1)
+            top = jnp.max(s, axis=1, keepdims=True)
+            p = jnp.exp(s - top).astype(BF)
+            o = lax.dot_general(p, vv, (((1,), (0,)), ((), ())), preferred_element_type=F32)
+            o_rows.append(o / pltpu.roll(o, DH, 1))
+            s_rows.append(top + jnp.log(o))
+        outs.append(jnp.concatenate(o_rows, axis=0))
+        stats.append(jnp.concatenate(s_rows, axis=0))
+    o_ref[...] = jnp.where(low_lanes, outs[0], outs[1]).astype(BF)
+    lse_ref[...] = jnp.where(low_lanes, stats[1], stats[0])
+
+
+def split3(value):
+    a = value.astype(BF)
+    rest = value - a.astype(F32)
+    b = rest.astype(BF)
+    c = (rest - b.astype(F32)).astype(BF)
+    return a, b, c
+
+
+def with_stat(base, value, lane):
+    a, b, c = split3(-value)
+    at = lane & (DH - 1)
+    base = jnp.where(at == STAT, a, base)
+    base = jnp.where(at == STAT + 1, b, base)
+    return jnp.where(at == STAT + 2, c, base)
+
+
+def attend_back_kernel(
+    causal,
+    q_ref, k_ref, v_ref, ko_ref, vo_ref, qf_ref, kf_ref, kfo_ref, o_ref, lse_ref, do_ref,
+    dq_ref, dk_ref, dv_ref, dko_ref, dvo_ref,
+):
+    size = q_ref.shape[0]
+    half = size // 2
+    lane = lax.broadcasted_iota(jnp.int32, (size, PAIR), 1)
+    low_lanes = lane < DH
+    scale = DH ** (-0.5)
+    q = q_ref[...] * jnp.array(scale, BF)
+    qf, kf, kfo = qf_ref[...], kf_ref[...], kfo_ref[...]
+    k, v, ko, vo = k_ref[...], v_ref[...], ko_ref[...], vo_ref[...]
+    do = do_ref[...]
+    product = do.astype(F32) * o_ref[...].astype(F32)
+    qstat = with_stat(qf, lse_ref[...], lane)
+    kall = jnp.concatenate([k, ko], axis=0)
+    zero = jnp.zeros_like(do)
+    dqs, dks, dvs = [], [], []
+    for head in range(2):
+        mine = low_lanes if head == 0 else jnp.logical_not(low_lanes)
+        inner = jnp.sum(jnp.where(mine, product, 0.0), axis=1, keepdims=True)
+        dstat = with_stat(zero, jnp.broadcast_to(inner, product.shape), lane)
+        qa = jnp.where(mine, q, qstat)
+        da = jnp.where(mine, do, dstat)
+        ka = jnp.concatenate([jnp.where(mine, k, kf), jnp.where(mine, ko, kfo)], axis=0)
+        va = jnp.concatenate([jnp.where(mine, v, kf), jnp.where(mine, vo, kfo)], axis=0)
+        if causal:
+            pieces = [
+                (0, half, [(0, half), (size, size + half)], 0),
+                (half, size, [(0, 2 * size)], half),
+            ]
+        else:
+            pieces = [(0, size, [(0, 2 * size)], None)]
+        dq_rows = []
+        dk_parts = [None] * 4
+        dv_parts = [None] * 4
+        for start, stop, spans, diagonal in pieces:
+            kk = jnp.concatenate([ka[a:b] for a, b in spans], axis=0)
+            vv = jnp.concatenate([va[a:b] for a, b in spans], axis=0)
+            kp = jnp.concatenate([kall[a:b] for a, b in spans], axis=0)
+            s = lax.dot_general(
+                kk, qa[start:stop], (((1,), (1,)), ((), ())), preferred_element_type=F32
+            )
+            if diagonal is not None:
+                row = lax.broadcasted_iota(jnp.int32, (half, half), 0)
+                col = lax.broadcasted_iota(jnp.int32, (half, half), 1)
+                cut = jnp.where(row <= col, s[diagonal : diagonal + half], NEGATIVE)
+                s = replace_block(s, cut, diagonal, 0)
+            p = jnp.exp(s)
+            dp = lax.dot_general(
+                vv, da[start:stop], (((1,), (1,)), ((), ())), preferred_element_type=F32
+            )
+            ds = (p * dp).astype(BF)
+            pb = p.astype(BF)
+            dv = lax.dot_general(
+                pb, do[start:stop], (((1,), (0,)), ((), ())), preferred_element_type=F32
+            )
+            dk = lax.dot_general(
+                ds, q[start:stop], (((1,), (0,)), ((), ())), preferred_element_type=F32
+            )
+            dq = lax.dot_general(
+                ds, kp, (((0,), (0,)), ((), ())), preferred_element_type=F32
+            )
+            dq_rows.append(dq * scale)
+            at = 0
+            for a, b in spans:
+                for block in range(a // half, b // half):
+                    rows = slice(at, at + half)
+                    dk_parts[block] = (
+                        dk[rows] if dk_parts[block] is None else dk_parts[block] + dk[rows]
+                    )
+                    dv_parts[block] = (
+                        dv[rows] if dv_parts[block] is None else dv_parts[block] + dv[rows]
+                    )
+                    at += half
+        dqs.append(jnp.concatenate(dq_rows, axis=0))
+        dks.append(jnp.concatenate(dk_parts, axis=0))
+        dvs.append(jnp.concatenate(dv_parts, axis=0))
+    dq_ref[...] = jnp.where(low_lanes, dqs[0], dqs[1]).astype(BF)
+    dk_ref[...] = jnp.where(low_lanes, dks[0][:size], dks[1][:size])
+    dv_ref[...] = jnp.where(low_lanes, dvs[0][:size], dvs[1][:size])
+    dko_ref[...] = jnp.where(low_lanes, dks[0][size:], dks[1][size:]).astype(BF)
+    dvo_ref[...] = jnp.where(low_lanes, dvs[0][size:], dvs[1][size:]).astype(BF)
+
+
+def column(size, at):
+    return pl.BlockSpec((size, PAIR), lambda p: (0, at + p))
+
+
+def shared(size):
+    return pl.BlockSpec((size, PAIR), lambda p: (0, 0))
+
+
+def attend_forward(q, k, v, ko, vo, qf, kf, kfo, causal):
+    size = q[0].shape[0]
+    steps = 8 // 2
+    width = steps * PAIR
+    return pl.pallas_call(
+        functools.partial(attend_kernel, causal),
+        grid=(steps,),
+        in_specs=[column(size, x[1]) for x in (q, k, v, ko, vo)] + [shared(size)] * 3,
+        out_specs=[column(size, 0)] * 2,
+        out_shape=[
+            jax.ShapeDtypeStruct((size, width), BF),
+            jax.ShapeDtypeStruct((size, width), F32),
+        ],
+        compiler_params=pltpu.CompilerParams(vmem_limit_bytes=48 << 20),
+        cost_estimate=pl.CostEstimate(
+            flops=16 * size * size * width, bytes_accessed=16 * size * width, transcendentals=0
+        ),
+        name="attend_forward",
+    )(q[0], k[0], v[0], ko[0], vo[0], qf, kf, kfo)
+
+
+def attend_backward(q, k, v, ko, vo, qf, kf, kfo, o, lse, do, causal):
+    size = q[0].shape[0]
+    steps = 8 // 2
+    width = steps * PAIR
+    return pl.pallas_call(
+        functools.partial(attend_back_kernel, causal),
+        grid=(steps,),
+        in_specs=[column(size, x[1]) for x in (q, k, v, ko, vo)]
+        + [shared(size)] * 3
+        + [column(size, 0)] * 3,
+        out_specs=[column(size, 0)] * 5,
+        out_shape=[
+            jax.ShapeDtypeStruct((size, width), BF),
+            jax.ShapeDtypeStruct((size, width), F32),
+            jax.ShapeDtypeStruct((size, width), F32),
+            jax.ShapeDtypeStruct((size, width), BF),
+            jax.ShapeDtypeStruct((size, width), BF),
+        ],
+        compiler_params=pltpu.CompilerParams(vmem_limit_bytes=48 << 20),
+        cost_estimate=pl.CostEstimate(
+            flops=40 * size * size * width, bytes_accessed=30 * size * width, transcendentals=0
+        ),
+        name="attend_backward",
+    )(q[0], k[0], v[0], ko[0], vo[0], qf, kf, kfo, o, lse, do)
+
+
+def dot(a, b):
+    return lax.dot_general(a, b, (((1,), (0,)), ((), ())), preferred_element_type=F32)
+
+
+def dot_back(a, b):
+    return lax.dot_general(a, b, (((1,), (1,)), ((), ())), preferred_element_type=F32)
+
+
+def dot_outer(a, b):
+    return lax.dot_general(a, b, (((0,), (0,)), ((), ())), preferred_element_type=F32)
+
+
+def sum_over_all(part, core, group, depth, to_cores):
+    rows = part.shape[0]
+    half = rows // 2
+
+    def take(value, at, count):
+        return lax.dynamic_slice_in_dim(value, at * count, count, 0)
+
+    def across(value, first):
+        def move(c, g, z):
+            return (c, g ^ (1 if (c == 0) == first else 2), z)
+
+        return swap(value, move)
+
+    along1 = functools.partial(swap, move=lambda c, g, z: (c, g, z ^ 1))
+    along2 = functools.partial(swap, move=lambda c, g, z: (c, g, z ^ 2))
+    bit_x, bit_y = group & 1, group >> 1
+    bits = [
+        core,
+        jnp.where(core == 0, bit_x, bit_y),
+        jnp.where(core == 0, bit_y, bit_x),
+        depth & 1,
+        depth >> 1,
+    ]
+    moves = [
+        to_core,
+        functools.partial(across, first=True),
+        functools.partial(across, first=False),
+        along1,
+        along2,
+    ]
+    value = part
+    count = rows
+    for bit, move in zip(bits, moves):
+        count //= 2
+        arrived = move(take(value, 1 - bit, count))
+        value = (take(value, bit, count).astype(F32) + arrived.astype(F32)).astype(BF)
+    for bit, move in list(zip(bits, moves))[:0:-1]:
+        arrived = move(value)
+        value = jnp.where(
+            bit == 0,
+            jnp.concatenate([value, arrived], axis=0),
+            jnp.concatenate([arrived, value], axis=0),
+        )
+    return value
+
+
+def join_cores(value, core, from_core):
+    if from_core is None:
+        arrived = to_core(value)
+    else:
+        arrived = swap(value, lambda c, g, z: (1 - c, g, z) if c == from_core else None)
+    return jnp.where(
+        core == 0,
+        jnp.concatenate([value, arrived], axis=0),
+        jnp.concatenate([arrived, value], axis=0),
+    )
+
+
+def row_shards(
+    inputs,
+    cotangent,
+    qkv_weight,
+    out_weight,
+    up_weight,
+    down_weight,
+    norm_gain,
+    norm_bias,
+    cross_q_weight,
+    cross_kv_weight,
+    cross_out_weight,
+    cross_gain,
+    cross_bias,
+    source_segments,
+    target_segments,
+):
+    core = lax.axis_index("section")
+    group = lax.axis_index("dp")
+    depth = lax.axis_index("seq")
+    tokens = inputs[0]
+    span = tokens.shape[1]
+    width = tokens.shape[2]
+    seat = 2 * core + (depth >> 1)
+
+    arrived = []
+    for k in range(4):
+        block = lax.dynamic_index_in_dim(tokens, seat ^ k, 0, keepdims=False)
+        arrived.append(
+            swap(block, lambda c, g, z: (side_of(z), g, (2 * c + (z >> 1)) ^ k))
+        )
+    blocks = pick(arrived, depth)
+    xs = jnp.concatenate(blocks[:2], axis=0)
+    xt = jnp.concatenate(blocks[2:], axis=0)
+
+    own = (qkv_weight[0], out_weight[0], up_weight[0], down_weight[0], norm_gain[0], norm_bias[0])
+    other = tuple(to_core(w) for w in own)
+    wqkv_e, wo_e, wu_e, wd_e, g_e, b_e = (jnp.where(core == 0, a, b) for a, b in zip(own, other))
+    wqkv_d, wo_d, wu_d, wd_d, g_d, b_d = (jnp.where(core == 0, b, a) for a, b in zip(own, other))
+
+    cots = []
+    for k in range(2):
+        block = lax.dynamic_index_in_dim(cotangent, seat ^ k, 0, keepdims=False)
+        cots.append(swap(block, lambda c, g, z: (side_of(z), g, (2 * c + (z >> 1)) ^ k)))
+    odd = (depth & 1) == 1
+    cot = jnp.concatenate(
+        [jnp.where(odd, cots[1], cots[0]), jnp.where(odd, cots[0], cots[1])], axis=0
+    ).astype(F32)
+
+    seg_s = lax.dynamic_index_in_dim(source_segments, depth, 0, keepdims=False).reshape(4, span)
+    seg_t = lax.dynamic_index_in_dim(target_segments, depth, 0, keepdims=False).reshape(4, span)
+
+    def in_order(seg):
+        outer, inner = seg[jnp.array([0, 3])].reshape(-1), seg[jnp.array([1, 2])].reshape(-1)
+        return jnp.where(core == 0, outer, inner), jnp.where(core == 0, inner, outer)
+
+    lane = lax.broadcasted_iota(jnp.int32, (2 * span, PAIR), 1) & (DH - 1)
+    late = lax.broadcasted_iota(jnp.int32, (2 * span, PAIR), 0) >= span
+
+    def query_features(seg):
+        hit = (seg[:, None] == lane) & (lane < 4)
+        hit = hit | ((lane == 4) & ~late) | ((lane == 5) & late)
+        return hit.astype(BF)
+
+    def key_features(seg, barred):
+        bad = ((seg[:, None] != lane) & (lane < 4)) | barred
+        value = jnp.where(bad, NEGATIVE, 0.0)
+        return jnp.where((lane >= STAT) & (lane < STAT + 3), 1.0, value).astype(BF)
+
+    none = jnp.zeros(lane.shape, bool)
+    seg_s0, seg_s1 = in_order(seg_s)
+    seg_t0, seg_t1 = in_order(seg_t)
+    qf_s, qf_t = query_features(seg_s0), query_features(seg_t0)
+    kf_s0, kf_s1 = key_features(seg_s0, none), key_features(seg_s1, none)
+    kf_t0 = key_features(seg_t0, (lane == 4) & late)
+    kf_t1 = key_features(
+        seg_t1, ((lane == 4) & (late | (core == 0))) | ((lane == 5) & late & (core == 1))
+    )
+
+    qkv_s = dot(xs, wqkv_e).astype(BF)
+    kv_s1 = to_core(qkv_s[:, width:])
+    qkv_t = dot(xt, wqkv_d).astype(BF)
+    kv_t1 = to_core(qkv_t[:, width:])
+    arg_s = ((qkv_s, 0), (qkv_s, 4), (qkv_s, 8), (kv_s1, 0), (kv_s1, 4), qf_s, kf_s0, kf_s1)
+    o_s, lse_s = attend_forward(*arg_s, False)
+    s1 = xs.astype(F32) + dot(o_s, wo_e)
+    h_s = layer_norm(s1, g_e[0], b_e[0])
+    h_s_low = h_s.astype(BF)
+    u_s = dot(h_s_low, wu_e)
+    gel_s = gelu_tanh(u_s).astype(BF)
+    s2 = h_s + dot(gel_s, wd_e)
+    memory = layer_norm(s2, g_e[1], b_e[1]).astype(BF)
+    ckv = dot(memory, cross_kv_weight).astype(BF)
+    ckv1 = to_core(ckv)
+
+    arg_t = ((qkv_t, 0), (qkv_t, 4), (qkv_t, 8), (kv_t1, 0), (kv_t1, 4), qf_t, kf_t0, kf_t1)
+    o_t, lse_t = attend_forward(*arg_t, True)
+    t1 = xt.astype(F32) + dot(o_t, wo_d)
+    h_t = layer_norm(t1, g_d[0], b_d[0])
+    h_t_low = h_t.astype(BF)
+    cq = dot(h_t_low, cross_q_weight).astype(BF)
+    arg_c = ((cq, 0), (ckv, 0), (ckv, 4), (ckv1, 0), (ckv1, 4), qf_t, kf_s0, kf_s1)
+    o_c, lse_c = attend_forward(*arg_c, False)
+    t2 = h_t + dot(o_c, cross_out_weight)
+    c_t = layer_norm(t2, cross_gain, cross_bias)
+    c_t_low = c_t.astype(BF)
+    u_t = dot(c_t_low, wu_d)
+    gel_t = gelu_tanh(u_t).astype(BF)
+    t3 = c_t + dot(gel_t, wd_d)
+    decoded, pull_t3 = jax.vjp(layer_norm, t3, g_d[1], b_d[1])
+    decoded = decoded.astype(BF)
+
+    grad_t3, gg_d1, gb_d1 = pull_t3(cot)
+    low_t3 = grad_t3.astype(BF)
+    gw_down_d = dot_outer(gel_t, low_t3)
+    grad_u_t = jax.vjp(gelu_tanh, u_t)[1](dot_back(low_t3, wd_d))[0].astype(BF)
+    gw_up_d = dot_outer(c_t_low, grad_u_t)
+    grad_c = grad_t3 + dot_back(grad_u_t, wu_d)
+    grad_t2, gg_c, gb_c = jax.vjp(layer_norm, t2, cross_gain, cross_bias)[1](grad_c)
+    low_t2 = grad_t2.astype(BF)
+    gw_cross_out = dot_outer(o_c, low_t2)
+    grad_o_c = dot_back(low_t2, cross_out_weight).astype(BF)
+    grad_cq, gk, gv, gk1, gv1 = attend_backward(*arg_c, o_c, lse_c, grad_o_c, False)
+    gkv1 = to_core(jnp.concatenate([gk1, gv1], axis=1))
+    grad_ckv = (jnp.concatenate([gk, gv], axis=1) + gkv1.astype(F32)).astype(BF)
+    gw_cross_q = dot_outer(h_t_low, grad_cq)
+    grad_h = grad_t2 + dot_back(grad_cq, cross_q_weight)
+    grad_t1, gg_d0, gb_d0 = jax.vjp(layer_norm, t1, g_d[0], b_d[0])[1](grad_h)
+    low_t1 = grad_t1.astype(BF)
+    gw_out_d = dot_outer(o_t, low_t1)
+    grad_o_t = dot_back(low_t1, wo_d).astype(BF)
+    gq, gk, gv, gk1, gv1 = attend_backward(*arg_t, o_t, lse_t, grad_o_t, True)
+    gkv1 = to_core(jnp.concatenate([gk1, gv1], axis=1))
+    grad_kv = (jnp.concatenate([gk, gv], axis=1) + gkv1.astype(F32)).astype(BF)
+    grad_qkv_t = jnp.concatenate([gq, grad_kv], axis=1)
+    gw_qkv_d = dot_outer(xt, grad_qkv_t)
+    grad_xt = grad_t1 + dot_back(grad_qkv_t, wqkv_d)
+
+    gw_cross_kv = dot_outer(memory, grad_ckv)
+    grad_memory = dot_back(grad_ckv, cross_kv_weight).astype(BF).astype(F32)
+    grad_s2, gg_e1, gb_e1 = jax.vjp(layer_norm, s2, g_e[1], b_e[1])[1](grad_memory)
+    low_s2 = grad_s2.astype(BF)
+    gw_down_e = dot_outer(gel_s, low_s2)
+    grad_u_s = jax.vjp(gelu_tanh, u_s)[1](dot_back(low_s2, wd_e))[0].astype(BF)
+    gw_up_e = dot_outer(h_s_low, grad_u_s)
+    grad_h = grad_s2 + dot_back(grad_u_s, wu_e)
+    grad_s1, gg_e0, gb_e0 = jax.vjp(layer_norm, s1, g_e[0], b_e[0])[1](grad_h)
+    low_s1 = grad_s1.astype(BF)
+    gw_out_e = dot_outer(o_s, low_s1)
+    grad_o_s = dot_back(low_s1, wo_e).astype(BF)
+    gq, gk, gv, gk1, gv1 = attend_backward(*arg_s, o_s, lse_s, grad_o_s, False)
+    gkv1 = to_core(jnp.concatenate([gk1, gv1], axis=1))
+    grad_kv = (jnp.concatenate([gk, gv], axis=1) + gkv1.astype(F32)).astype(BF)
+    grad_qkv_s = jnp.concatenate([gq, grad_kv], axis=1)
+    gw_qkv_e = dot_outer(xs, grad_qkv_s)
+    grad_xs = grad_s1 + dot_back(grad_qkv_s, wqkv_e)
+
+    def home(source, target):
+        parts = [source[:span], source[span:], target[:span], target[span:]]
+        sent = pick(parts, depth)
+        back = [
+            swap(
+                sent[k],
+                lambda c, g, z: ((z ^ k) >> 1, g, block_of(c, (z ^ k) & 1)),
+            )
+            for k in range(4)
+        ]
+        return jnp.stack(pick(back, seat))
+
+    outputs = home(memory, decoded)
+    grads = home(grad_xs.astype(BF), grad_xt.astype(BF)).astype(F32)
+
+    def fold(value):
+        return value.reshape(-1, width, value.shape[1])
+
+    def pack(parts):
+        return jnp.concatenate([p.astype(BF) for p in parts], axis=1)
+
+    def down_columns(value):
+        return [value[i * width : (i + 1) * width] for i in range(value.shape[0] // width)]
+
+    ffn_d = pack([gw_up_d] + down_columns(gw_down_d))
+    rest_d = pack([gw_cross_out, gw_cross_q, gw_out_d, gw_qkv_d])
+    ffn_e = pack([gw_cross_kv, gw_up_e] + down_columns(gw_down_e))
+    rest_e = pack([gw_out_e, gw_qkv_e])
+    ffn_d, rest_d, ffn_e, rest_e = (
+        sum_over_all(v, core, group, depth, None) for v in (ffn_d, rest_d, ffn_e, rest_e)
+    )
+    kv_at = cross_kv_weight.shape[1]
+    shared_part = join_cores(
+        jnp.concatenate([rest_d[:, : 2 * width], ffn_e[:, :kv_at]], axis=1), core, None
+    )
+    mine = jnp.where(
+        core == 0,
+        jnp.concatenate([ffn_e[:, kv_at:], rest_e], axis=1),
+        jnp.concatenate([ffn_d, rest_d[:, 2 * width :]], axis=1),
+    )
+    theirs = jnp.where(
+        core == 0,
+        jnp.concatenate([ffn_d, rest_d[:, 2 * width :]], axis=1),
+        jnp.concatenate([ffn_e[:, kv_at:], rest_e], axis=1),
+    )
+    lacking = to_core(theirs)
+    whole = jnp.where(
+        core == 0,
+        jnp.concatenate([mine, lacking], axis=0),
+        jnp.concatenate([lacking, mine], axis=0),
+    ).astype(F32)
+    shared_part = shared_part.astype(F32)
+    ff = up_weight.shape[2]
+    g_up = whole[:, :ff]
+    g_down = jnp.concatenate(
+        [whole[:, ff + i * width : ff + (i + 1) * width] for i in range(ff // width)], axis=0
+    )
+    g_out = whole[:, 2 * ff : 2 * ff + width]
+    g_qkv = whole[:, 2 * ff + width :]
+    g_cross_out = shared_part[:, :width]
+    g_cross_q = shared_part[:, width : 2 * width]
+    g_cross_kv = shared_part[:, 2 * width :]
+
+    small = jnp.stack(
+        [gg_e0, gg_e1, gb_e0, gb_e1, gg_d0, gg_d1, gb_d0, gb_d1, gg_c, gb_c]
+        + [jnp.zeros_like(gg_c)] * 6
+    )
+    for move in (
+        to_core,
+        functools.partial(swap, move=lambda c, g, z: (c, g ^ 1, z)),
+        functools.partial(swap, move=lambda c, g, z: (c, g ^ 2, z)),
+        functools.partial(swap, move=lambda c, g, z: (c, g, z ^ 1)),
+        functools.partial(swap, move=lambda c, g, z: (c, g, z ^ 2)),
+    ):
+        small = small + move(small)
+    layer_small = jnp.where(core == 0, small[:4], small[4:8])
+    return (
+        outputs[None],
+        grads[None],
+        g_qkv[None],
+        g_out[None],
+        g_up[None],
+        g_down[None],
+        layer_small[None, :2],
+        layer_small[None, 2:],
+        g_cross_q,
+        g_cross_kv,
+        g_cross_out,
+        small[8],
+        small[9],
+    )
+
+
 def solution(mesh):
     in_specs = (
         P("section", "dp", "seq", None),
@@ -441,4 +1015,6 @@
         P(),
         P(),
     )
-    return jax.shard_map(shards, mesh=mesh, in_specs=in_specs, out_specs=out_specs, check_vma=False)
+    whole_rows = mesh.shape["section"] == 2 and mesh.shape["seq"] == 4 and mesh.shape["dp"] == 4
+    body = row_shards if whole_rows else shards
+    return jax.shard_map(body, mesh=mesh, in_specs=in_specs, out_specs=out_specs, check_vma=False)

time: 1760 us -> 483 us (0.27)
  waiting for transfers between devices: 997 us -> 143 us
  matrix products: 424 us -> 74 us
  local copies, waits for them, and re-layouts: 149 us -> 32.4 us
  starting transfers between devices: 10.6 us -> 103 us
  blocking collectives: 74.6 us -> 0 us
  Pallas kernels: 0 us -> 66.5 us
  other arithmetic: 83.9 us -> 54.8 us
    psum x2 -> x0, waiting for transfers between devices: 425 us -> none  [the longest x1 369 us: shards(): lax.psum((totals[0], totals[1], totals[2], totals[3], totals[4], totals[5...]
    all_gather x12 -> x0, waiting for transfers between devices: 335 us -> none  [the longest x6 200 us: attend_keys(): lax.all_gather(value_rows, 'seq', axis=1, tiled=True)]
    dot_general x91 -> x33, matrix products: 359 us -> 74 us  [the longest x11 30.9 us: dot_back(): lax.dot_general(a, b, (((1,), (1,)), ((), ())), preferred_element_type=F32)]
    reduce_scatter x10 -> x0, waiting for transfers between devices: 226 us -> none  [the longest x5 137 us: attend_back(): lax.psum_scatter(joined_view(part_values).astype(jnp.bfloat16), 'seq', sc...]
    ppermute x4 -> x69, waiting for transfers between devices: 7.2 us -> 143 us  [swap(): return lax.ppermute(value, AXES, pairs)]
    ppermute x4 -> x69, starting transfers between devices: 8.41 us -> 103 us  [swap(): return lax.ppermute(value, AXES, pairs)]
    psum x2 -> x0, blocking collectives: 74.6 us -> none  [the longest x1 40.1 us: shards(): lax.psum((totals[6], totals[7], totals[8], totals[9], totals[10]), ('sect...]
    pallas_call x0 -> x6, Pallas kernels: none -> 66.5 us  [the longest x3 40.7 us: attend_backward(): pl.pallas_call(functools.partial(attend_back_kernel, causal), grid=(steps...]
  transfers between devices with their start and end apart: 28 -> 69, of which waited for: 23 -> 32; matrix products, arithmetic and copies ran while one was open for 25% -> 23% of each run, Pallas kernels for 0% -> 9%
where the time goes in v1:
time: 483 us; the launch traced here: 477 us
  waiting for transfers between devices  143 us (30%)
  starting transfers between devices  103 us (21%)
  matrix products  74 us (15%)
  Pallas kernels  66.5 us (14%)
  other arithmetic  54.8 us (11%)
  local copies, waits for them, and re-layouts  32.4 us (7%)
    ppermute x69, waiting for transfers between devices, swap(): return lax.ppermute(value, AXES, pairs)  143 us
    ppermute x69, starting transfers between devices, swap(): return lax.ppermute(value, AXES, pairs)  103 us
    pallas_call x3, Pallas kernels, attend_backward(): pl.pallas_call(functools.partial(attend_back_kernel, causal), grid=(steps...  40.7 us
    dot_general x11, matrix products, dot_back(): lax.dot_general(a, b, (((1,), (1,)), ((), ())), preferred_element_type=F32)  30.9 us
    dot_general x11, matrix products, dot(): lax.dot_general(a, b, (((1,), (0,)), ((), ())), preferred_element_type=F32)  26.5 us
    pallas_call x3, Pallas kernels, attend_forward(): pl.pallas_call(functools.partial(attend_kernel, causal), grid=(steps,), i...  25.9 us
    dot_general x11, matrix products, dot_outer(): lax.dot_general(a, b, (((0,), (0,)), ((), ())), preferred_element_type=F32)  16.6 us
    select_n x16, other arithmetic, sum_over_all(): jnp.where(bit == 0, jnp.concatenate([value, arrived], axis=0), jnp.concat...  10.5 us
  transfers between devices with their start and end apart: 69, of which 32 were waited for; matrix products, arithmetic and copies ran while one was open for 23% of the time, Pallas kernels for 9%

profile of v1, /device:TPU:1, one launch (start us, length us, event | category | flops | bytes accessed | tf_op | source)
XLA Modules:
  0.0 477.4 jit_solution(5527677831490102909)
XLA Ops:
  3.4 5.6 %collective-permute-start.3 = (bf16[256,512]{0,1:T(8,128)(2,1)}, bf16[256,512]{0,1:T(8,128)(2,1)}, u32[]{:S(2)}, u32[]{:S(2)}) collective-permute-start(bf16[256,512]{0,1:T(8,128)(2,1)} %bitcast.3), channel_id=1, source_target_pairs={{0,0},{1,16},{2,17},{3,1},{4,4},{5,20},{6,21},{7,5},{8,8},{9,24},{... | collective-permute-start | bytes 786440 | tf_op jit(solution)/shard_map/ppermute | solution.py:432
  24.5 4.5 collective-permute-start.18
  29.0 4.1 collective-permute-start.17
  33.2 4.6 collective-permute-done.2
  48.8 8.9 %attend_forward.3 = (bf16[512,512]{1,0:T(8,128)(2,1)S(1)}, f32[512,512]{1,0:T(8,128)S(1)}) custom-call(bf16[512,1536]{1,0:T(8,128)(2,1)S(1)} %convolution_convert_fusion.3.q_ref.k_ref.v_ref, bf16[512,1536]{1,0:T(8,128)(2,1)S(1)} %convolution_convert_fusion.3.q_ref.k_ref.v_ref, bf16[512,1536]{1,0:T(8,128)(2,1)S(1)} %convolution_convert_fusion.3.q_ref.k_ref.v_ref, ...), custom_call_target="tpu_custom_call" | custom-call | flops 2147483648 | bytes 4194304 | tf_op jit(solution)/shard_map/attend_forward/pallas_call | solution.py:622
  60.0 3.9 fusion.37
  64.0 5.8 %fusion.98 = (f32[512]{0:T(512)S(1)}, f32[512,512]{0,1:T(8,128)S(1)}) fusion(bf16[2048,512]{1,0:T(8,128)(2,1)} %collective-permute-done.10, pred[]{:T(512)S(6)} %eq.48, bf16[1,2048,512]{2,1,0:T(8,128)(2,1)} %param.24, f32[512,2048]{1,0:T(8,128)S(1)} %fusion.37, f32[512]{0:T(512)S(1)} %bitcast.184, f32[512]{0:T(512)S(1)} %bitcast.179, f32[512]{0:T(512)S(1)} %fusion.49, ...), kind=kOutput, calls=%fused_computation.361 | convolution fusion | flops 1085799936 | bytes 10496001 | tf_op jit(solution)/shard_map/dot_general | solution.py:666
  71.1 7.9 %attend_forward.4 = (bf16[512,512]{1,0:T(8,128)(2,1)S(1)}, f32[512,512]{1,0:T(8,128)S(1)}) custom-call(bf16[512,1536]{1,0:T(8,128)(2,1)S(1)} %convolution_convert_fusion.2.q_ref.k_ref.v_ref, bf16[512,1536]{1,0:T(8,128)(2,1)S(1)} %convolution_convert_fusion.2.q_ref.k_ref.v_ref, bf16[512,1536]{1,0:T(8,128)(2,1)S(1)} %convolution_convert_fusion.2.q_ref.k_ref.v_ref, ...), custom_call_target="tpu_custom_call" | custom-call | flops 2147483648 | bytes 4194304 | tf_op jit(solution)/shard_map/attend_forward/pallas_call | solution.py:622
  82.0 9.0 %attend_forward.5 = (bf16[512,512]{1,0:T(8,128)(2,1)S(1)}, f32[512,512]{1,0:T(8,128)S(1)}) custom-call(bf16[512,512]{1,0:T(8,128)(2,1)S(1)} %convolution_convert_fusion.17.q_ref, bf16[512,1024]{1,0:T(8,128)(2,1)S(1)} %convolution_convert_fusion.9.k_ref.v_ref, bf16[512,1024]{1,0:T(8,128)(2,1)S(1)} %convolution_convert_fusion.9.k_ref.v_ref, ...), custom_call_target="tpu_custom_call" | custom-call | flops 2147483648 | bytes 4194304 | tf_op jit(solution)/shard_map/attend_forward/pallas_call | solution.py:622
  103.2 6.2 %fusion.14 = bf16[512,2048]{1,0:T(8,128)(2,1)S(1)} fusion(f32[512,2048]{1,0:T(8,128)S(1)} %fusion.38, bf16[2048,512]{1,0:T(8,128)(2,1)} %collective-permute-done.10, pred[]{:T(512)S(6)} %eq.48, f32[512,512]{0,1:T(8,128)S(1)} %get-tuple-element.91, f32[512]{0:T(512)S(1)} %negate_multiply_fusion.4, bf16[1,2048,512]{2,1,0:T(8,128)(2,1)} %param.24), kind=kOutput, calls=%fused_computation.24 | convolution fusion | flops 1096286208 | bytes 11536385 | tf_op jit(solution)/shard_map/dot_general | solution.py:670
  109.4 4.6 multiply_reduce_fusion
  114.8 14.2 %attend_backward.3 = (bf16[512,512]{1,0:T(8,128)(2,1)S(1)}, f32[512,512]{1,0:T(8,128)S(1)}, f32[512,512]{1,0:T(8,128)S(1)}, bf16[512,512]{1,0:T(8,128)(2,1)S(1)}, bf16[512,512]{1,0:T(8,128)(2,1)S(1)}) custom-call(bf16[512,512]{1,0:T(8,128)(2,1)S(1)} %convolution_convert_fusion.17.q_ref, bf16[512,1024]{1,0:T(8,128)(2,1)} %copy-done.12, ...), custom_call_target="tpu_custom_call" | custom-call | flops 5368709120 | bytes 7864320 | tf_op jit(solution)/shard_map/attend_backward/pallas_call | solution.py:643
  133.2 4.9 %collective-permute-start.15 = (bf16[256,512]{0,1:T(8,128)(2,1)S(1)}, bf16[256,512]{0,1:T(8,128)(2,1)S(1)}, u32[]{:S(2)}, u32[]{:S(2)}) collective-permute-start(bf16[256,512]{0,1:T(8,128)(2,1)S(1)} %get-tuple-element.116), channel_id=1, source_target_pairs={{0,3},{1,0},{2,19},{3,16},{4,7},{5,4},{6,23},{7,20},{8,11},{9,8},{... | collective-permute-start | bytes 786440 | tf_op jit(solution)/shard_map/ppermute | solution.py:432
  142.0 5.1 %collective-permute-start.16 = (bf16[256,512]{0,1:T(8,128)(2,1)S(1)}, bf16[256,512]{0,1:T(8,128)(2,1)S(1)}, u32[]{:S(2)}, u32[]{:S(2)}) collective-permute-start(bf16[256,512]{0,1:T(8,128)(2,1)S(1)} %get-tuple-element.119), channel_id=1, source_target_pairs={{0,0},{1,3},{2,16},{3,19},{4,4},{5,7},{6,20},{7,23},{8,8},{9,11},{... | collective-permute-start | bytes 786440 | tf_op jit(solution)/shard_map/ppermute | solution.py:432
  152.7 9.0 %collective-permute-done.16 = bf16[256,512]{0,1:T(8,128)(2,1)S(1)} collective-permute-done((bf16[256,512]{0,1:T(8,128)(2,1)S(1)}, bf16[256,512]{0,1:T(8,128)(2,1)S(1)}, u32[]{:S(2)}, u32[]{:S(2)}) %collective-permute-start.16) | collective-permute-done | bytes 262176 | tf_op jit(solution)/shard_map/ppermute | solution.py:432
  170.0 6.4 %fusion.7 = bf16[512,2048]{1,0:T(8,128)(2,1)S(1)} fusion(f32[512,2048]{1,0:T(8,128)S(1)} %copy-done.35, bf16[2048,512]{1,0:T(8,128)(2,1)} %collective-permute-done.10, pred[]{:T(512)S(6)} %eq.48, f32[512]{0:T(512)S(1)} %negate_multiply_fusion.2, bf16[1,2048,512]{2,1,0:T(8,128)(2,1)} %param.24, bf16[512,512]{0,1:T(8,128)(2,1)S(1)} %get-tuple-element.167, ...), kind=kOutput, calls=%fused_computation.17 | convolution fusion | flops 1098121216 | bytes 12068865 | tf_op jit(solution)/shard_map/dot_general | solution.py:670
  176.4 4.1 multiply_reduce_fusion.2
  188.2 12.2 %attend_backward.5 = (bf16[512,512]{1,0:T(8,128)(2,1)S(1)}, f32[512,512]{1,0:T(8,128)S(1)}, f32[512,512]{1,0:T(8,128)S(1)}, bf16[512,512]{1,0:T(8,128)(2,1)S(1)}, bf16[512,512]{1,0:T(8,128)(2,1)S(1)}) custom-call(bf16[512,1536]{1,0:T(8,128)(2,1)} %copy-done.3, bf16[512,1536]{1,0:T(8,128)(2,1)} %copy-done.3, bf16[512,1536]{1,0:T(8,128)(2,1)} %copy-done.3, ...), custom_call_target="tpu_custom_call" | custom-call | flops 5368709120 | bytes 7864320 | tf_op jit(solution)/shard_map/attend_backward/pallas_call | solution.py:643
  203.3 14.3 %attend_backward.4 = (bf16[512,512]{1,0:T(8,128)(2,1)S(1)}, f32[512,512]{1,0:T(8,128)S(1)}, f32[512,512]{1,0:T(8,128)S(1)}, bf16[512,512]{1,0:T(8,128)(2,1)S(1)}, bf16[512,512]{1,0:T(8,128)(2,1)S(1)}) custom-call(bf16[512,1536]{1,0:T(8,128)(2,1)} %copy-done.2, bf16[512,1536]{1,0:T(8,128)(2,1)} %copy-done.2, bf16[512,1536]{1,0:T(8,128)(2,1)} %copy-done.2, ...), custom_call_target="tpu_custom_call" | custom-call | flops 5368709120 | bytes 7864320 | tf_op jit(solution)/shard_map/attend_backward/pallas_call | solution.py:643
  249.4 5.1 %collective-permute-done.45 = bf16[128,4096]{1,0:T(8,128)(2,1)S(1)} collective-permute-done((bf16[128,4096]{1,0:T(8,128)(2,1)S(1)}, bf16[128,4096]{1,0:T(8,128)(2,1)S(1)}, u32[]{:S(2)}, u32[]{:S(2)}) %collective-permute-start.45) | collective-permute-done | bytes 1048608 | tf_op jit(solution)/shard_map/ppermute | solution.py:432
  256.0 4.0 collective-permute-done.36
  284.3 6.0 %collective-permute-done.40 = bf16[16,2048]{1,0:T(8,128)(2,1)S(1)} collective-permute-done((bf16[16,2048]{1,0:T(8,128)(2,1)S(1)}, bf16[16,2048]{1,0:T(8,128)(2,1)S(1)}, u32[]{:S(2)}, u32[]{:S(2)}) %collective-permute-start.40) | collective-permute-done | bytes 65568 | tf_op jit(solution)/shard_map/ppermute | solution.py:432
  305.8 15.5 %collective-permute-done.28 = bf16[64,5120]{1,0:T(8,128)(2,1)S(1)} collective-permute-done((bf16[64,5120]{1,0:T(8,128)(2,1)S(1)}, bf16[64,5120]{1,0:T(8,128)(2,1)S(1)}, u32[]{:S(2)}, u32[]{:S(2)}) %collective-permute-start.28) | collective-permute-done | bytes 655392 | tf_op jit(solution)/shard_map/ppermute | solution.py:432
  321.7 6.1 %collective-permute-done.29 = bf16[32,5120]{1,0:T(8,128)(2,1)S(1)} collective-permute-done((bf16[32,5120]{1,0:T(8,128)(2,1)S(1)}, bf16[32,5120]{1,0:T(8,128)(2,1)S(1)}, u32[]{:S(2)}, u32[]{:S(2)}) %collective-permute-start.29) | collective-permute-done | bytes 327712 | tf_op jit(solution)/shard_map/ppermute | solution.py:432
  330.4 5.3 %collective-permute-done.30 = bf16[16,5120]{1,0:T(8,128)(2,1)S(1)} collective-permute-done((bf16[16,5120]{1,0:T(8,128)(2,1)S(1)}, bf16[16,5120]{1,0:T(8,128)(2,1)S(1)}, u32[]{:S(2)}, u32[]{:S(2)}) %collective-permute-start.30) | collective-permute-done | bytes 163872 | tf_op jit(solution)/shard_map/ppermute | solution.py:432
  343.8 7.2 %collective-permute-done.32 = bf16[32,5120]{1,0:T(8,128)(2,1)S(1)} collective-permute-done((bf16[32,5120]{1,0:T(8,128)(2,1)S(1)}, bf16[32,5120]{1,0:T(8,128)(2,1)S(1)}, u32[]{:S(2)}, u32[]{:S(2)}) %collective-permute-start.32) | collective-permute-done | bytes 327712 | tf_op jit(solution)/shard_map/ppermute | solution.py:432
  356.1 4.5 collective-permute-done.33
  376.1 24.9 %collective-permute-done.61 = bf16[128,3072]{1,0:T(8,128)(2,1)} collective-permute-done((bf16[128,3072]{1,0:T(8,128)(2,1)}, bf16[128,3072]{1,0:T(8,128)(2,1)}, u32[]{:S(2)}, u32[]{:S(2)}) %collective-permute-start.61) | collective-permute-done | bytes 786464 | tf_op jit(solution)/shard_map/ppermute | solution.py:432
  409.6 8.5 %collective-permute-start.62 = (bf16[256,6144]{1,0:T(8,128)(2,1)}, bf16[256,6144]{1,0:T(8,128)(2,1)}, u32[]{:S(2)}, u32[]{:S(2)}) collective-permute-start(bf16[256,6144]{1,0:T(8,128)(2,1)} %get-tuple-element.98), channel_id=1, source_target_pairs={{0,16},{1,17},{2,18},{3,19},{4,20},{5,21},{6,22},{7,23},{8,24},{9,... | collective-permute-start | bytes 9437192 | tf_op jit(solution)/shard_map/ppermute | solution.py:432
  438.4 10.6 %collective-permute-done.25 = bf16[256,512]{0,1:T(8,128)(2,1)S(1)} collective-permute-done((bf16[256,512]{0,1:T(8,128)(2,1)S(1)}, bf16[256,512]{0,1:T(8,128)(2,1)S(1)}, u32[]{:S(2)}, u32[]{:S(2)}) %collective-permute-start.25) | collective-permute-done | bytes 262176 | tf_op jit(solution)/shard_map/ppermute | solution.py:432
  451.1 8.6 %fusion.20 = f32[512,2048]{1,0:T(8,128)S(1)} fusion(bf16[256,2048]{1,0:T(8,128)(2,1)} %collective-permute-done.68, bf16[256,1024]{1,0:T(8,128)(2,1)S(1)} %slice.245, bf16[256,1024]{1,0:T(8,128)(2,1)S(1)} %slice.244, pred[]{:T(512)S(6)} %eq.48), kind=kLoop, calls=%fused_computation.61 | loop fusion | flops 14680064 | bytes 6291457 | tf_op jit(solution)/shard_map/convert_element_type | solution.py:943
  463.8 4.8 fusion
  (510 shorter events, 227.6 us)
Async XLA Ops:
  0.7 19.1 %collective-permute-start.8 = (f32[2,512]{1,0:T(2,128)}, f32[2,512]{1,0:T(2,128)S(1)}, u32[]{:S(2)}, u32[]{:S(2)}) collective-permute-start(f32[2,512]{1,0:T(2,128)} %bitcast.215), channel_id=1, source_target_pairs={{0,16},{1,17},{2,18},{3,19},{4,20},{5,21},{6,22},{7,23},{8,24},{9,... | collective-permute-start | bytes 12296 | tf_op jit(solution)/shard_map/ppermute | solution.py:432
  0.8 21.0 %collective-permute-start.7 = (f32[2,512]{1,0:T(2,128)}, f32[2,512]{1,0:T(2,128)}, u32[]{:S(2)}, u32[]{:S(2)}) collective-permute-start(f32[2,512]{1,0:T(2,128)} %bitcast.216), channel_id=1, source_target_pairs={{0,16},{1,17},{2,18},{3,19},{4,20},{5,21},{6,22},{7,23},{8,24},{9,... | collective-permute-start | bytes 12296 | tf_op jit(solution)/shard_map/ppermute | solution.py:432
  3.4 21.1 %collective-permute-start.3 = (bf16[256,512]{0,1:T(8,128)(2,1)}, bf16[256,512]{0,1:T(8,128)(2,1)}, u32[]{:S(2)}, u32[]{:S(2)}) collective-permute-start(bf16[256,512]{0,1:T(8,128)(2,1)} %bitcast.3), channel_id=1, source_target_pairs={{0,0},{1,16},{2,17},{3,1},{4,4},{5,20},{6,21},{7,5},{8,8},{9,24},{... | collective-permute-start | bytes 786440 | tf_op jit(solution)/shard_map/ppermute | solution.py:432
  9.8 19.2 %collective-permute-start = (bf16[256,512]{0,1:T(8,128)(2,1)}, bf16[256,512]{0,1:T(8,128)(2,1)}, u32[]{:S(2)}, u32[]{:S(2)}) collective-permute-start(bf16[256,512]{0,1:T(8,128)(2,1)} %bitcast), channel_id=1, source_target_pairs={{0,3},{1,19},{2,18},{3,2},{4,7},{5,23},{6,22},{7,6},{8,11},{9,27},... | collective-permute-start | bytes 786440 | tf_op jit(solution)/shard_map/ppermute | solution.py:432
  11.8 27.2 %collective-permute-start.4 = (bf16[512,1536]{1,0:T(8,128)(2,1)}, bf16[512,1536]{1,0:T(8,128)(2,1)}, u32[]{:S(2)}, u32[]{:S(2)}) collective-permute-start(bf16[512,1536]{1,0:T(8,128)(2,1)} %bitcast.224), channel_id=1, source_target_pairs={{0,16},{1,17},{2,18},{3,19},{4,20},{5,21},{6,22},{7,23},{8,24},{9,... | collective-permute-start | bytes 4718600 | tf_op jit(solution)/shard_map/ppermute | solution.py:432
  21.8 16.0 %collective-permute-start.2 = (bf16[256,512]{0,1:T(8,128)(2,1)S(1)}, bf16[256,512]{0,1:T(8,128)(2,1)S(1)}, u32[]{:S(2)}, u32[]{:S(2)}) collective-permute-start(bf16[256,512]{0,1:T(8,128)(2,1)S(1)} %bitcast.176), channel_id=1, source_target_pairs={{0,1},{1,17},{2,16},{3,0},{4,5},{5,21},{6,20},{7,4},{8,9},{9,25},{... | collective-permute-start | bytes 786440 | tf_op jit(solution)/shard_map/ppermute | solution.py:432
  24.5 18.0 %collective-permute-start.18 = (bf16[256,512]{0,1:T(8,128)(2,1)S(1)}, bf16[256,512]{0,1:T(8,128)(2,1)S(1)}, u32[]{:S(2)}, u32[]{:S(2)}) collective-permute-start(bf16[256,512]{0,1:T(8,128)(2,1)S(1)} %bitcast.175), channel_id=1, source_target_pairs={{0,0},{1,16},{2,17},{3,1},{4,4},{5,20},{6,21},{7,5},{8,8},{9,24},{... | collective-permute-start | bytes 786440 | tf_op jit(solution)/shard_map/ppermute | solution.py:432
  29.0 17.4 %collective-permute-start.17 = (bf16[256,512]{0,1:T(8,128)(2,1)S(1)}, bf16[256,512]{0,1:T(8,128)(2,1)S(1)}, u32[]{:S(2)}, u32[]{:S(2)}) collective-permute-start(bf16[256,512]{0,1:T(8,128)(2,1)S(1)} %bitcast.174), channel_id=1, source_target_pairs={{0,1},{1,17},{2,16},{3,0},{4,5},{5,21},{6,20},{7,4},{8,9},{9,25},{... | collective-permute-start | bytes 786440 | tf_op jit(solution)/shard_map/ppermute | solution.py:432
  33.1 24.7 %collective-permute-start.6 = (bf16[512,512]{1,0:T(8,128)(2,1)}, bf16[512,512]{1,0:T(8,128)(2,1)S(1)}, u32[]{:S(2)}, u32[]{:S(2)}) collective-permute-start(bf16[512,512]{1,0:T(8,128)(2,1)} %bitcast.5), channel_id=1, source_target_pairs={{0,16},{1,17},{2,18},{3,19},{4,20},{5,21},{6,22},{7,23},{8,24},{9,... | collective-permute-start | bytes 1572872 | tf_op jit(solution)/shard_map/ppermute | solution.py:432
  37.8 22.2 %collective-permute-start.9 = (bf16[512,2048]{1,0:T(8,128)(2,1)}, bf16[512,2048]{1,0:T(8,128)(2,1)S(1)}, u32[]{:S(2)}, u32[]{:S(2)}) collective-permute-start(bf16[512,2048]{1,0:T(8,128)(2,1)} %bitcast.10), channel_id=1, source_target_pairs={{0,16},{1,17},{2,18},{3,19},{4,20},{5,21},{6,22},{7,23},{8,24},{9,... | collective-permute-start | bytes 6291464 | tf_op jit(solution)/shard_map/ppermute | solution.py:432
  42.5 21.5 %collective-permute-start.10 = (bf16[2048,512]{1,0:T(8,128)(2,1)}, bf16[2048,512]{1,0:T(8,128)(2,1)}, u32[]{:S(2)}, u32[]{:S(2)}) collective-permute-start(bf16[2048,512]{1,0:T(8,128)(2,1)} %bitcast.11), channel_id=1, source_target_pairs={{0,16},{1,17},{2,18},{3,19},{4,20},{5,21},{6,22},{7,23},{8,24},{9,... | collective-permute-start | bytes 6291464 | tf_op jit(solution)/shard_map/ppermute | solution.py:432
  48.8 22.3 %collective-permute-start.11 = (bf16[512,1024]{1,0:T(8,128)(2,1)}, bf16[512,1024]{1,0:T(8,128)(2,1)S(1)}, u32[]{:S(2)}, u32[]{:S(2)}) collective-permute-start(bf16[512,1024]{1,0:T(8,128)(2,1)} %slice.212), channel_id=1, source_target_pairs={{0,16},{1,17},{2,18},{3,19},{4,20},{5,21},{6,22},{7,23},{8,24},{9,... | collective-permute-start | bytes 3145736 | tf_op jit(solution)/shard_map/ppermute | solution.py:432
  133.2 18.1 %collective-permute-start.15 = (bf16[256,512]{0,1:T(8,128)(2,1)S(1)}, bf16[256,512]{0,1:T(8,128)(2,1)S(1)}, u32[]{:S(2)}, u32[]{:S(2)}) collective-permute-start(bf16[256,512]{0,1:T(8,128)(2,1)S(1)} %get-tuple-element.116), channel_id=1, source_target_pairs={{0,3},{1,0},{2,19},{3,16},{4,7},{5,4},{6,23},{7,20},{8,11},{9,8},{... | collective-permute-start | bytes 786440 | tf_op jit(solution)/shard_map/ppermute | solution.py:432
  142.0 19.7 %collective-permute-start.16 = (bf16[256,512]{0,1:T(8,128)(2,1)S(1)}, bf16[256,512]{0,1:T(8,128)(2,1)S(1)}, u32[]{:S(2)}, u32[]{:S(2)}) collective-permute-start(bf16[256,512]{0,1:T(8,128)(2,1)S(1)} %get-tuple-element.119), channel_id=1, source_target_pairs={{0,0},{1,3},{2,16},{3,19},{4,4},{5,7},{6,20},{7,23},{8,8},{9,11},{... | collective-permute-start | bytes 786440 | tf_op jit(solution)/shard_map/ppermute | solution.py:432
  151.3 86.6 %collective-permute-start.44 = (bf16[256,4096]{1,0:T(8,128)(2,1)}, bf16[256,4096]{1,0:T(8,128)(2,1)}, u32[]{:S(2)}, u32[]{:S(2)}) collective-permute-start(bf16[256,4096]{1,0:T(8,128)(2,1)} %constant_dynamic-slice_fusion.9), channel_id=1, source_target_pairs={{0,16},{1,17},{2,18},{3,19},{4,20},{5,21},{6,22},{7,23},{8,24},{9,... | collective-permute-start | bytes 6291464 | tf_op jit(solution)/shard_map/ppermute | solution.py:432
  183.9 37.6 %collective-permute-start.63 = (f32[16,512]{1,0:T(8,128)}, f32[16,512]{1,0:T(8,128)S(1)}, u32[]{:S(2)}, u32[]{:S(2)}) collective-permute-start(f32[16,512]{1,0:T(8,128)} %stack.61), channel_id=1, source_target_pairs={{0,16},{1,17},{2,18},{3,19},{4,20},{5,21},{6,22},{7,23},{8,24},{9,... | collective-permute-start | bytes 98312 | tf_op jit(solution)/shard_map/ppermute | solution.py:432
  200.7 41.1 %collective-permute-start.21 = (bf16[512,1024]{1,0:T(8,128)(2,1)S(1)}, bf16[512,1024]{1,0:T(8,128)(2,1)}, u32[]{:S(2)}, u32[]{:S(2)}) collective-permute-start(bf16[512,1024]{1,0:T(8,128)(2,1)S(1)} %pad_maximum_fusion.7), channel_id=1, source_target_pairs={{0,16},{1,17},{2,18},{3,19},{4,20},{5,21},{6,22},{7,23},{8,24},{9,... | collective-permute-start | bytes 3145736 | tf_op jit(solution)/shard_map/ppermute | solution.py:432
  217.8 16.3 %collective-permute-start.20 = (bf16[512,1024]{1,0:T(8,128)(2,1)S(1)}, bf16[512,1024]{1,0:T(8,128)(2,1)S(1)}, u32[]{:S(2)}, u32[]{:S(2)}) collective-permute-start(bf16[512,1024]{1,0:T(8,128)(2,1)S(1)} %pad_maximum_fusion.6), channel_id=1, source_target_pairs={{0,16},{1,17},{2,18},{3,19},{4,20},{5,21},{6,22},{7,23},{8,24},{9,... | collective-permute-start | bytes 3145736 | tf_op jit(solution)/shard_map/ppermute | solution.py:432
  228.4 40.3 %collective-permute-start.26 = (bf16[256,5120]{1,0:T(8,128)(2,1)S(1)}, bf16[256,5120]{1,0:T(8,128)(2,1)S(1)}, u32[]{:S(2)}, u32[]{:S(2)}) collective-permute-start(bf16[256,5120]{1,0:T(8,128)(2,1)S(1)} %constant_dynamic-slice_fusion.18), channel_id=1, source_target_pairs={{0,16},{1,17},{2,18},{3,19},{4,20},{5,21},{6,22},{7,23},{8,24},{9,... | collective-permute-start | bytes 7864328 | tf_op jit(solution)/shard_map/ppermute | solution.py:432
  231.5 140.8 %collective-permute-start.67 = (f32[16,512]{1,0:T(8,128)S(1)}, f32[16,512]{1,0:T(8,128)S(1)}, u32[]{:S(2)}, u32[]{:S(2)}) collective-permute-start(f32[16,512]{1,0:T(8,128)S(1)} %add.408), channel_id=1, source_target_pairs={{0,2},{1,3},{2,0},{3,1},{4,6},{5,7},{6,4},{7,5},{8,10},{9,11},{10,... | collective-permute-start | bytes 98312 | tf_op jit(solution)/shard_map/ppermute | solution.py:432
  262.2 35.0 %collective-permute-start.54 = (bf16[128,3072]{1,0:T(8,128)(2,1)S(1)}, bf16[128,3072]{1,0:T(8,128)(2,1)S(1)}, u32[]{:S(2)}, u32[]{:S(2)}) collective-permute-start(bf16[128,3072]{1,0:T(8,128)(2,1)S(1)} %constant_dynamic-slice_fusion.3), channel_id=1, source_target_pairs={{0,4},{1,5},{2,6},{3,7},{4,0},{5,1},{6,2},{7,3},{8,12},{9,13},{10,... | collective-permute-start | bytes 2359304 | tf_op jit(solution)/shard_map/ppermute | solution.py:432
  269.8 34.3 %collective-permute-start.27 = (bf16[128,5120]{1,0:T(8,128)(2,1)S(1)}, bf16[128,5120]{1,0:T(8,128)(2,1)S(1)}, u32[]{:S(2)}, u32[]{:S(2)}) collective-permute-start(bf16[128,5120]{1,0:T(8,128)(2,1)S(1)} %constant_dynamic-slice_fusion.17), channel_id=1, source_target_pairs={{0,4},{1,5},{2,6},{3,7},{4,0},{5,1},{6,2},{7,3},{8,12},{9,13},{10,... | collective-permute-start | bytes 3932168 | tf_op jit(solution)/shard_map/ppermute | solution.py:432
  301.5 51.1 %collective-permute-start.51 = (bf16[64,4096]{1,0:T(8,128)(2,1)S(1)}, bf16[64,4096]{1,0:T(8,128)(2,1)S(1)}, u32[]{:S(2)}, u32[]{:S(2)}) collective-permute-start(bf16[64,4096]{1,0:T(8,128)(2,1)S(1)} %maximum_select_fusion.11), channel_id=1, source_target_pairs={{0,8},{1,9},{2,10},{3,11},{4,12},{5,13},{6,14},{7,15},{8,0},{9,1},... | collective-permute-start | bytes 1572872 | tf_op jit(solution)/shard_map/ppermute | solution.py:432
  302.2 70.1 %collective-permute-start.43 = (bf16[128,2048]{1,0:T(8,128)(2,1)S(1)}, bf16[128,2048]{1,0:T(8,128)(2,1)}, u32[]{:S(2)}, u32[]{:S(2)}) collective-permute-start(bf16[128,2048]{1,0:T(8,128)(2,1)S(1)} %maximum_select_fusion.10), channel_id=1, source_target_pairs={{0,4},{1,5},{2,6},{3,7},{4,0},{5,1},{6,2},{7,3},{8,12},{9,13},{10,... | collective-permute-start | bytes 1572872 | tf_op jit(solution)/shard_map/ppermute | solution.py:432
  304.5 16.9 %collective-permute-start.28 = (bf16[64,5120]{1,0:T(8,128)(2,1)S(1)}, bf16[64,5120]{1,0:T(8,128)(2,1)S(1)}, u32[]{:S(2)}, u32[]{:S(2)}) collective-permute-start(bf16[64,5120]{1,0:T(8,128)(2,1)S(1)} %constant_dynamic-slice_fusion.16), channel_id=1, source_target_pairs={{0,8},{1,9},{2,10},{3,11},{4,12},{5,13},{6,14},{7,15},{8,0},{9,1},... | collective-permute-start | bytes 1966088 | tf_op jit(solution)/shard_map/ppermute | solution.py:432
  305.7 15.9 %collective-permute-start.56 = (bf16[32,3072]{1,0:T(8,128)(2,1)S(1)}, bf16[32,3072]{1,0:T(8,128)(2,1)S(1)}, u32[]{:S(2)}, u32[]{:S(2)}) collective-permute-start(bf16[32,3072]{1,0:T(8,128)(2,1)S(1)} %constant_dynamic-slice_fusion.1), channel_id=1, source_target_pairs={{0,1},{1,0},{2,3},{3,2},{4,5},{5,4},{6,7},{7,6},{8,9},{9,8},{10,11... | collective-permute-start | bytes 589832 | tf_op jit(solution)/shard_map/ppermute | solution.py:432
  352.9 21.0 %collective-permute-start.52 = (bf16[128,4096]{1,0:T(8,128)(2,1)S(1)}, bf16[128,4096]{1,0:T(8,128)(2,1)}, u32[]{:S(2)}, u32[]{:S(2)}) collective-permute-start(bf16[128,4096]{1,0:T(8,128)(2,1)S(1)} %maximum_select_fusion.7), channel_id=1, source_target_pairs={{0,4},{1,5},{2,6},{3,7},{4,0},{5,1},{6,2},{7,3},{8,12},{9,13},{10,... | collective-permute-start | bytes 3145736 | tf_op jit(solution)/shard_map/ppermute | solution.py:432
  360.9 42.7 %collective-permute-start.34 = (bf16[128,5120]{1,0:T(8,128)(2,1)S(1)}, bf16[128,5120]{1,0:T(8,128)(2,1)}, u32[]{:S(2)}, u32[]{:S(2)}) collective-permute-start(bf16[128,5120]{1,0:T(8,128)(2,1)S(1)} %maximum_select_fusion.5), channel_id=1, source_target_pairs={{0,4},{1,5},{2,6},{3,7},{4,0},{5,1},{6,2},{7,3},{8,12},{9,13},{10,... | collective-permute-start | bytes 3932168 | tf_op jit(solution)/shard_map/ppermute | solution.py:432
  366.1 34.9 %collective-permute-start.61 = (bf16[128,3072]{1,0:T(8,128)(2,1)}, bf16[128,3072]{1,0:T(8,128)(2,1)}, u32[]{:S(2)}, u32[]{:S(2)}) collective-permute-start(bf16[128,3072]{1,0:T(8,128)(2,1)} %maximum_select_fusion.8), channel_id=1, source_target_pairs={{0,4},{1,5},{2,6},{3,7},{4,0},{5,1},{6,2},{7,3},{8,12},{9,13},{10,... | collective-permute-start | bytes 2359304 | tf_op jit(solution)/shard_map/ppermute | solution.py:432
  409.6 53.0 %collective-permute-start.62 = (bf16[256,6144]{1,0:T(8,128)(2,1)}, bf16[256,6144]{1,0:T(8,128)(2,1)}, u32[]{:S(2)}, u32[]{:S(2)}) collective-permute-start(bf16[256,6144]{1,0:T(8,128)(2,1)} %get-tuple-element.98), channel_id=1, source_target_pairs={{0,16},{1,17},{2,18},{3,19},{4,20},{5,21},{6,22},{7,23},{8,24},{9,... | collective-permute-start | bytes 9437192 | tf_op jit(solution)/shard_map/ppermute | solution.py:432
  424.9 26.2 %collective-permute-start.68 = (bf16[256,2048]{1,0:T(8,128)(2,1)}, bf16[256,2048]{1,0:T(8,128)(2,1)}, u32[]{:S(2)}, u32[]{:S(2)}) collective-permute-start(bf16[256,2048]{1,0:T(8,128)(2,1)} %pad_maximum_fusion.8), channel_id=1, source_target_pairs={{0,16},{1,17},{2,18},{3,19},{4,20},{5,21},{6,22},{7,23},{8,24},{9,... | collective-permute-start | bytes 3145736 | tf_op jit(solution)/shard_map/ppermute | solution.py:432
  432.5 16.4 %collective-permute-start.25 = (bf16[256,512]{0,1:T(8,128)(2,1)S(1)}, bf16[256,512]{0,1:T(8,128)(2,1)S(1)}, u32[]{:S(2)}, u32[]{:S(2)}) collective-permute-start(bf16[256,512]{0,1:T(8,128)(2,1)S(1)} %get-tuple-element.109), channel_id=1, source_target_pairs={{0,0},{1,3},{2,16},{3,19},{4,4},{5,7},{6,20},{7,23},{8,8},{9,11},{... | collective-permute-start | bytes 786440 | tf_op jit(solution)/shard_map/ppermute | solution.py:432
  (130 other events, 1274.0 us)

commit v2 on v1

--- a/solution.py
+++ b/solution.py
@@ -460,7 +460,7 @@
     return jnp.concatenate(parts, axis=axis)
 
 
-def attend_kernel(causal, q_ref, k_ref, v_ref, ko_ref, vo_ref, qf_ref, kf_ref, kfo_ref, o_ref, lse_ref):
+def attend_kernel(causal, q_ref, k_ref, v_ref, ko_ref, vo_ref, qf_ref, kf_ref, kfo_ref, o_ref, of_ref, lse_ref):
     size = q_ref.shape[0]
     half = size // 2
     lane = lax.broadcasted_iota(jnp.int32, (size, PAIR), 1)
@@ -501,7 +501,9 @@
             s_rows.append(top + jnp.log(o))
         outs.append(jnp.concatenate(o_rows, axis=0))
         stats.append(jnp.concatenate(s_rows, axis=0))
-    o_ref[...] = jnp.where(low_lanes, outs[0], outs[1]).astype(BF)
+    whole = jnp.where(low_lanes, outs[0], outs[1])
+    o_ref[...] = whole.astype(BF)
+    of_ref[...] = whole
     lse_ref[...] = jnp.where(low_lanes, stats[1], stats[0])
 
 
@@ -535,7 +537,7 @@
     qf, kf, kfo = qf_ref[...], kf_ref[...], kfo_ref[...]
     k, v, ko, vo = k_ref[...], v_ref[...], ko_ref[...], vo_ref[...]
     do = do_ref[...]
-    product = do.astype(F32) * o_ref[...].astype(F32)
+    product = do.astype(F32) * o_ref[...]
     qstat = with_stat(qf, lse_ref[...], lane)
     kall = jnp.concatenate([k, ko], axis=0)
     zero = jnp.zeros_like(do)
@@ -623,9 +625,10 @@
         functools.partial(attend_kernel, causal),
         grid=(steps,),
         in_specs=[column(size, x[1]) for x in (q, k, v, ko, vo)] + [shared(size)] * 3,
-        out_specs=[column(size, 0)] * 2,
+        out_specs=[column(size, 0)] * 3,
         out_shape=[
             jax.ShapeDtypeStruct((size, width), BF),
+            jax.ShapeDtypeStruct((size, width), F32),
             jax.ShapeDtypeStruct((size, width), F32),
         ],
         compiler_params=pltpu.CompilerParams(vmem_limit_bytes=48 << 20),
@@ -674,62 +677,448 @@
     return lax.dot_general(a, b, (((0,), (0,)), ((), ())), preferred_element_type=F32)
 
 
-def sum_over_all(part, core, group, depth, to_cores):
-    rows = part.shape[0]
-    half = rows // 2
-
-    def take(value, at, count):
-        return lax.dynamic_slice_in_dim(value, at * count, count, 0)
-
-    def across(value, first):
-        def move(c, g, z):
-            return (c, g ^ (1 if (c == 0) == first else 2), z)
-
-        return swap(value, move)
-
-    along1 = functools.partial(swap, move=lambda c, g, z: (c, g, z ^ 1))
-    along2 = functools.partial(swap, move=lambda c, g, z: (c, g, z ^ 2))
-    bit_x, bit_y = group & 1, group >> 1
+MESH = pl.DeviceIdType.MESH
+
+
+def place():
+    core = lax.axis_index("section")
+    group = lax.axis_index("dp")
+    depth = lax.axis_index("seq")
+    return core, group, depth, ((depth + 1) // 2) % 2, depth // 2
+
+
+def greet(others):
+    barrier = pltpu.get_barrier_semaphore()
+    for other in others:
+        pl.semaphore_signal(barrier, inc=1, device_id=other, device_id_type=MESH)
+    pl.semaphore_wait(barrier, len(others))
+
+
+def row_mates(core, group, depth):
+    mates = [(1 - core, group, depth)]
+    for step in range(1, 4):
+        there = (depth + step) % 4
+        mates += [(core, group, there), (1 - core, group, there)]
+    return mates
+
+
+def remote(source, target, send, recv, device):
+    return pltpu.make_async_remote_copy(
+        src_ref=source,
+        dst_ref=target,
+        send_sem=send,
+        recv_sem=recv,
+        device_id=device,
+        device_id_type=MESH,
+    )
+
+
+def spread_kernel(count, x_ref, *refs):
+    weights, (x_out, *outs) = refs[:count], refs[count : 2 * count + 1]
+    refs = refs[2 * count + 1 :]
+    x_held, held = refs[0], refs[1 : count + 1]
+    x_send, x_recv, x_own, w_send, w_recv, w_own, w_out = refs[count + 1 :]
+    core, group, depth, side, at = place()
+    span = x_ref.shape[1]
+    loads = [pltpu.make_async_copy(weights[i], held[i], w_own.at[i]) for i in range(count)]
+    for load in loads:
+        load.start()
+    x_load = pltpu.make_async_copy(x_ref.at[depth], x_held, x_own)
+    x_load.start()
+    greet(row_mates(core, group, depth))
+    seat = 2 * core + at
+    copies = []
+    for step in (2, 1, 3, 0):
+        row = (depth + step) % 4
+        target = x_out.at[core, pl.ds(pl.multiple_of(at * span, span), span)]
+        if step == 0:
+            there = remote(
+                x_held, target, x_send.at[step], x_recv.at[seat], (side, group, row)
+            )
+            here = pltpu.make_async_copy(x_held, target, x_recv.at[seat])
+            x_load.wait()
+
+            @pl.when(side == core)
+            def _():
+                here.start()
+
+            @pl.when(side != core)
+            def _():
+                there.start()
+        else:
+            there = remote(
+                x_ref.at[row], target, x_send.at[step], x_recv.at[seat], (side, group, row)
+            )
+            there.start()
+        copies.append((step, there))
+    moves = []
+    for i in range(count):
+        loads[i].wait()
+        own = pltpu.make_async_copy(held[i], outs[i].at[core], w_out.at[i])
+        gone = remote(
+            held[i], outs[i].at[core], w_send.at[i], w_recv.at[i], (1 - core, group, depth)
+        )
+        gone.start()
+        own.start()
+        moves.append((own, gone))
+    for own, gone in moves:
+        own.wait()
+        gone.wait()
+    for step, there in copies:
+        if step == 0:
+
+            @pl.when(side != core)
+            def _():
+                there.wait_send()
+        else:
+            there.wait_send()
+    for seat_from in range(4):
+        target = x_out.at[seat_from // 2, pl.ds((seat_from % 2) * span, span)]
+        pltpu.make_async_copy(x_held, target, x_recv.at[seat_from]).wait()
+
+
+def spread(tokens, *weights):
+    rows, span, width = tokens.shape
+    count = len(weights)
+    anywhere = pl.BlockSpec(memory_space=pl.ANY)
+    dma = pltpu.SemaphoreType.DMA
+    return pl.pallas_call(
+        functools.partial(spread_kernel, count),
+        in_specs=[anywhere] * (count + 1),
+        out_specs=[anywhere] * (count + 1),
+        out_shape=[jax.ShapeDtypeStruct((2, 2 * span, width), BF)]
+        + [jax.ShapeDtypeStruct((2,) + w.shape, w.dtype) for w in weights],
+        scratch_shapes=[pltpu.VMEM((span, width), BF)]
+        + [pltpu.VMEM(w.shape, w.dtype) for w in weights]
+        + [dma((4,)), dma((4,)), dma]
+        + [dma((count,))] * 4,
+        compiler_params=pltpu.CompilerParams(collective_id=0, has_side_effects=True),
+        name="spread",
+    )(tokens, *weights)
+
+
+def gradient_groups(width, hidden):
+    folds = hidden // width
+    groups = []
+    for layer, up, down in ((1, 0, 1), (0, 2, 3)):
+        groups.append((layer, [(up, 0, hidden)]))
+        groups.append((layer, [(down, i * width, width) for i in range(folds)]))
+    groups.append((1, [(4, 0, width), (5, 0, 3 * width)]))
+    groups.append((0, [(6, 0, width), (7, 0, 3 * width)]))
+    groups.append((None, [(8, 0, width), (9, 0, width)]))
+    groups.append((None, [(10, 0, 2 * width)]))
+    return groups
+
+
+RESULT_OF = (0, 1, 0, 1, 2, 3, 2, 3, 4, 5, 6)
+
+
+def collect_kernel(groups, *refs):
+    blocks = refs[:4]
+    parts = refs[4:15]
+    small = refs[15]
+    home = refs[16:18]
+    results = refs[18:25]
+    small_out = refs[25]
+    (
+        own, got0, got1, got2, got3, got4, total, small_got,
+        home_send, home_recv, own_sem, send0, recv0, send, recv, small_send, small_recv, out_sem,
+    ) = refs[26:]
+    core, group, depth, side, at = place()
+    partner = (1 - core, group, depth)
+    x_next = group + 1 - 2 * (group % 2)
+    y_next = (group + 2) % 4
+    first = x_next + core * (y_next - x_next)
+    second = y_next + core * (x_next - y_next)
+    z_next = depth + 1 - 2 * (depth % 2)
+    z_far = (depth + 2) % 4
+    neighbours = [
+        partner,
+        (core, first, depth),
+        (core, second, depth),
+        (core, group, z_next),
+        (core, group, z_far),
+    ]
+    greet(row_mates(core, group, depth) + neighbours[1:3])
+    bit_x, bit_y = group % 2, group // 2
     bits = [
         core,
-        jnp.where(core == 0, bit_x, bit_y),
-        jnp.where(core == 0, bit_y, bit_x),
-        depth & 1,
-        depth >> 1,
+        bit_x + core * (bit_y - bit_x),
+        bit_y + core * (bit_x - bit_y),
+        depth % 2,
+        depth // 2,
     ]
-    moves = [
-        to_core,
-        functools.partial(across, first=True),
-        functools.partial(across, first=False),
-        along1,
-        along2,
-    ]
-    value = part
-    count = rows
-    for bit, move in zip(bits, moves):
+    got = [got0, got1, got2, got3, got4]
+    half = got0.shape[0]
+    span = blocks[0].shape[0] // 2
+
+    first_row = [core * half]
+    count = half
+    for k in range(1, 5):
         count //= 2
-        arrived = move(take(value, 1 - bit, count))
-        value = (take(value, bit, count).astype(F32) + arrived.astype(F32)).astype(BF)
-    for bit, move in list(zip(bits, moves))[:0:-1]:
-        arrived = move(value)
-        value = jnp.where(
-            bit == 0,
-            jnp.concatenate([value, arrived], axis=0),
-            jnp.concatenate([arrived, value], axis=0),
+        first_row.append(first_row[-1] + bits[k] * count)
+
+    starts = []
+    column = 0
+    for _, pieces in groups:
+        starts.append(column)
+        column += sum(p[2] for p in pieces)
+    widths = [sum(p[2] for p in pieces) for _, pieces in groups]
+
+    def rows(first, count):
+        return pl.ds(pl.multiple_of(first, 16), count)
+
+    def columns(g):
+        return pl.ds(starts[g], widths[g])
+
+    def step0(g):
+        column = starts[g]
+        copies = []
+        for i, (array, row, wide) in enumerate(groups[g][1]):
+            away = parts[array].at[rows(row + (1 - core) * half, half)]
+            copy = remote(
+                away, got0.at[:, pl.ds(column, wide)], send0.at[g, i], recv0.at[g, i], partner
+            )
+            copy.start()
+            copies.append(copy)
+            column += wide
+        for copy in locals_of(g):
+            copy.start()
+        return copies
+
+    def locals_of(g):
+        column = starts[g]
+        found = []
+        for i, (array, row, wide) in enumerate(groups[g][1]):
+            here = parts[array].at[rows(row + core * half, half)]
+            found.append(
+                pltpu.make_async_copy(here, own.at[:, pl.ds(column, wide)], own_sem.at[g, i])
+            )
+            column += wide
+        return found
+
+    def add(target, source, first, g):
+        count = target.shape[0]
+        strip = 16
+
+        @pl.loop(0, count // strip)
+        def _(i):
+            r = pl.multiple_of(i * strip, strip)
+            mine = source[pl.ds(pl.multiple_of(first + r, strip), strip), columns(g)]
+            theirs = target[pl.ds(r, strip), columns(g)]
+            target[pl.ds(r, strip), columns(g)] = (
+                mine.astype(F32) + theirs.astype(F32)
+            ).astype(BF)
+
+    pending = {}
+
+    def halving(g, k):
+        count = got[k].shape[0]
+        source = got[k - 1].at[rows((1 - bits[k]) * count, count), columns(g)]
+        copy = remote(
+            source, got[k].at[:, columns(g)], send.at[g, k], recv.at[g, k], neighbours[k]
         )
-    return value
-
-
-def join_cores(value, core, from_core):
-    if from_core is None:
-        arrived = to_core(value)
-    else:
-        arrived = swap(value, lambda c, g, z: (1 - c, g, z) if c == from_core else None)
-    return jnp.where(
-        core == 0,
-        jnp.concatenate([value, arrived], axis=0),
-        jnp.concatenate([arrived, value], axis=0),
-    )
+        copy.start()
+        return copy
+
+    def doubling(g, k):
+        count = got[k].shape[0]
+        block = total.at[rows(first_row[k], count), columns(g)]
+        copy = remote(block, block, send.at[g, 4 + k], recv.at[g, 4 + k], neighbours[k])
+        copy.start()
+        return copy
+
+    def joining(g):
+        layer = groups[g][0]
+        block = total.at[rows(core * half, half), columns(g)]
+        copy = remote(block, block, send.at[g, 9], recv.at[g, 9], partner)
+        if layer is None:
+            copy.start()
+        else:
+
+            @pl.when(core != layer)
+            def _():
+                copy.start()
+
+        return copy
+
+    def finish_join(g, copy):
+        layer, pieces = groups[g]
+        if layer is None:
+            copy.wait()
+        else:
+
+            @pl.when(core != layer)
+            def _():
+                copy.wait_send()
+
+            @pl.when(core == layer)
+            def _():
+                copy.wait_recv()
+
+    def emit(g, wait):
+        layer, pieces = groups[g]
+        column = starts[g]
+        for i, (array, row, wide) in enumerate(pieces):
+            copy = pltpu.make_async_copy(
+                total.at[:, pl.ds(column, wide)],
+                results[RESULT_OF[array]].at[pl.ds(row, 2 * half)],
+                out_sem.at[g, i],
+            )
+            column += wide
+            act = copy.wait if wait else copy.start
+            if layer is None:
+                act()
+            else:
+
+                @pl.when(core == layer)
+                def _():
+                    act()
+
+    steps = 11
+
+    def run(g, step):
+        if step == 0:
+            pending[g] = step0(g)
+            return
+        if step == 1:
+            for copy in pending[g]:
+                copy.wait()
+            for copy in locals_of(g):
+                copy.wait()
+            add(got0, own, 0, g)
+            pending[g] = halving(g, 1)
+            return
+        if step <= 5:
+            pending[g].wait()
+            k = step - 1
+            count = got[k].shape[0]
+            add(got[k], got[k - 1], bits[k] * count, g)
+            if step <= 4:
+                pending[g] = halving(g, step)
+                return
+            total[rows(first_row[4], count), columns(g)] = got4[:, columns(g)]
+            pending[g] = doubling(g, 4)
+            return
+        if step <= 8:
+            pending[g].wait()
+            pending[g] = doubling(g, 9 - step)
+            return
+        if step == 9:
+            pending[g].wait()
+            pending[g] = joining(g)
+            return
+        finish_join(g, pending[g])
+        emit(g, False)
+
+    def home_copy(a, j):
+        layer, where = j // 2, j % 2
+        there = 2 * where + (core + where) % 2
+        source = blocks[2 * a + layer].at[pl.ds(where * span, span)]
+        target = home[a].at[depth]
+        return (
+            remote(
+                source, target, home_send.at[a, j], home_recv.at[a, depth], (layer, group, there)
+            ),
+            pltpu.make_async_copy(source, target, home_recv.at[a, depth]),
+            (there == depth) & (core == layer),
+        )
+
+    def home_start(a, j):
+        far, near, stays = home_copy(a, j)
+
+        @pl.when(stays)
+        def _():
+            near.start()
+
+        @pl.when(jnp.logical_not(stays))
+        def _():
+            far.start()
+
+    def small_step(k):
+        if k > 0:
+            small_copy(k - 1).wait()
+            small_out[...] += small_got[k - 1]
+        else:
+            small_out[...] = small[...]
+        if k < 5:
+            small_copy(k).start()
+
+    def small_copy(k):
+        return remote(
+            small_out, small_got.at[k], small_send.at[k], small_recv.at[k], neighbours[k]
+        )
+
+    number = len(groups)
+    todo = [(a, j) for a in range(2) for j in range(4)]
+    for slot in range(number + steps - 1):
+        for g in range(number):
+            if 0 <= slot - g < steps:
+                run(g, slot - g)
+        if todo and slot >= 1:
+            home_start(*todo.pop(0))
+        if slot <= 5:
+            small_step(slot)
+    for g in range(number):
+        emit(g, True)
+    for a in range(2):
+        for j in range(4):
+            far, near, stays = home_copy(a, j)
+
+            @pl.when(jnp.logical_not(stays))
+            def _():
+                far.wait_send()
+
+            pltpu.make_async_copy(
+                blocks[0].at[pl.ds(0, span)], home[a].at[j], home_recv.at[a, j]
+            ).wait()
+
+
+def collect(outputs, grads, parts, small):
+    size, width = outputs[0].shape
+    hidden = parts[0].shape[1]
+    groups = gradient_groups(width, hidden)
+    wide = sum(p[2] for _, pieces in groups for p in pieces)
+    number = len(groups)
+    most = max(len(pieces) for _, pieces in groups)
+    half = width // 2
+    anywhere = pl.BlockSpec(memory_space=pl.ANY)
+    resident = pl.BlockSpec(memory_space=pltpu.VMEM)
+    dma = pltpu.SemaphoreType.DMA
+    shapes = [parts[i].shape for i in (0, 1, 4, 5, 8, 9, 10)]
+    out = pl.pallas_call(
+        functools.partial(collect_kernel, groups),
+        in_specs=[resident] * 4 + [anywhere] * 11 + [resident],
+        out_specs=[anywhere] * 9 + [resident],
+        out_shape=[jax.ShapeDtypeStruct((4, size // 2, width), BF)] * 2
+        + [jax.ShapeDtypeStruct(s, BF) for s in shapes]
+        + [jax.ShapeDtypeStruct(small.shape, F32)],
+        scratch_shapes=[
+            pltpu.VMEM((half, wide), BF),
+            pltpu.VMEM((half, wide), BF),
+            pltpu.VMEM((half // 2, wide), BF),
+            pltpu.VMEM((half // 4, wide), BF),
+            pltpu.VMEM((half // 8, wide), BF),
+            pltpu.VMEM((half // 16, wide), BF),
+            pltpu.VMEM((2 * half, wide), BF),
+            pltpu.VMEM((5,) + small.shape, F32),
+            dma((2, 4)),
+            dma((2, 4)),
+            dma((number, most)),
+            dma((number, most)),
+            dma((number, most)),
+            dma((number, 10)),
+            dma((number, 10)),
+            dma((5,)),
+            dma((5,)),
+            dma((number, most)),
+        ],
+        compiler_params=pltpu.CompilerParams(
+            collective_id=1, has_side_effects=True, vmem_limit_bytes=56 << 20
+        ),
+        name="collect",
+    )(*outputs, *grads, *parts, small)
+    return out[0], out[1], out[2:9], out[9]
 
 
 def row_shards(
@@ -750,27 +1139,27 @@
     target_segments,
 ):
     core = lax.axis_index("section")
-    group = lax.axis_index("dp")
     depth = lax.axis_index("seq")
-    tokens = inputs[0]
-    span = tokens.shape[1]
-    width = tokens.shape[2]
+    span = inputs.shape[2]
+    width = inputs.shape[3]
     seat = 2 * core + (depth >> 1)
 
-    arrived = []
-    for k in range(4):
-        block = lax.dynamic_index_in_dim(tokens, seat ^ k, 0, keepdims=False)
-        arrived.append(
-            swap(block, lambda c, g, z: (side_of(z), g, (2 * c + (z >> 1)) ^ k))
-        )
-    blocks = pick(arrived, depth)
-    xs = jnp.concatenate(blocks[:2], axis=0)
-    xt = jnp.concatenate(blocks[2:], axis=0)
-
-    own = (qkv_weight[0], out_weight[0], up_weight[0], down_weight[0], norm_gain[0], norm_bias[0])
-    other = tuple(to_core(w) for w in own)
-    wqkv_e, wo_e, wu_e, wd_e, g_e, b_e = (jnp.where(core == 0, a, b) for a, b in zip(own, other))
-    wqkv_d, wo_d, wu_d, wd_d, g_d, b_d = (jnp.where(core == 0, b, a) for a, b in zip(own, other))
+    x_both, qkv_both, out_both, up_both, down_both, gain_both, bias_both = spread(
+        inputs[0],
+        qkv_weight[0],
+        out_weight[0],
+        up_weight[0],
+        down_weight[0],
+        norm_gain[0],
+        norm_bias[0],
+    )
+    xs, xt = x_both[0], x_both[1]
+    wqkv_e, wo_e, wu_e, wd_e, g_e, b_e = (
+        w[0] for w in (qkv_both, out_both, up_both, down_both, gain_both, bias_both)
+    )
+    wqkv_d, wo_d, wu_d, wd_d, g_d, b_d = (
+        w[1] for w in (qkv_both, out_both, up_both, down_both, gain_both, bias_both)
+    )
 
     cots = []
     for k in range(2):
@@ -816,7 +1205,7 @@
     qkv_t = dot(xt, wqkv_d).astype(BF)
     kv_t1 = to_core(qkv_t[:, width:])
     arg_s = ((qkv_s, 0), (qkv_s, 4), (qkv_s, 8), (kv_s1, 0), (kv_s1, 4), qf_s, kf_s0, kf_s1)
-    o_s, lse_s = attend_forward(*arg_s, False)
+    o_s, of_s, lse_s = attend_forward(*arg_s, False)
     s1 = xs.astype(F32) + dot(o_s, wo_e)
     h_s = layer_norm(s1, g_e[0], b_e[0])
     h_s_low = h_s.astype(BF)
@@ -828,13 +1217,13 @@
     ckv1 = to_core(ckv)
 
     arg_t = ((qkv_t, 0), (qkv_t, 4), (qkv_t, 8), (kv_t1, 0), (kv_t1, 4), qf_t, kf_t0, kf_t1)
-    o_t, lse_t = attend_forward(*arg_t, True)
+    o_t, of_t, lse_t = attend_forward(*arg_t, True)
     t1 = xt.astype(F32) + dot(o_t, wo_d)
     h_t = layer_norm(t1, g_d[0], b_d[0])
     h_t_low = h_t.astype(BF)
     cq = dot(h_t_low, cross_q_weight).astype(BF)
     arg_c = ((cq, 0), (ckv, 0), (ckv, 4), (ckv1, 0), (ckv1, 4), qf_t, kf_s0, kf_s1)
-    o_c, lse_c = attend_forward(*arg_c, False)
+    o_c, of_c, lse_c = attend_forward(*arg_c, False)
     t2 = h_t + dot(o_c, cross_out_weight)
     c_t = layer_norm(t2, cross_gain, cross_bias)
     c_t_low = c_t.astype(BF)
@@ -854,7 +1243,7 @@
     low_t2 = grad_t2.astype(BF)
     gw_cross_out = dot_outer(o_c, low_t2)
     grad_o_c = dot_back(low_t2, cross_out_weight).astype(BF)
-    grad_cq, gk, gv, gk1, gv1 = attend_backward(*arg_c, o_c, lse_c, grad_o_c, False)
+    grad_cq, gk, gv, gk1, gv1 = attend_backward(*arg_c, of_c, lse_c, grad_o_c, False)
     gkv1 = to_core(jnp.concatenate([gk1, gv1], axis=1))
     grad_ckv = (jnp.concatenate([gk, gv], axis=1) + gkv1.astype(F32)).astype(BF)
     gw_cross_q = dot_outer(h_t_low, grad_cq)
@@ -863,7 +1252,7 @@
     low_t1 = grad_t1.astype(BF)
     gw_out_d = dot_outer(o_t, low_t1)
     grad_o_t = dot_back(low_t1, wo_d).astype(BF)
-    gq, gk, gv, gk1, gv1 = attend_backward(*arg_t, o_t, lse_t, grad_o_t, True)
+    gq, gk, gv, gk1, gv1 = attend_backward(*arg_t, of_t, lse_t, grad_o_t, True)
     gkv1 = to_core(jnp.concatenate([gk1, gv1], axis=1))
     grad_kv = (jnp.concatenate([gk, gv], axis=1) + gkv1.astype(F32)).astype(BF)
     grad_qkv_t = jnp.concatenate([gq, grad_kv], axis=1)
@@ -882,92 +1271,34 @@
     low_s1 = grad_s1.astype(BF)
     gw_out_e = dot_outer(o_s, low_s1)
     grad_o_s = dot_back(low_s1, wo_e).astype(BF)
-    gq, gk, gv, gk1, gv1 = attend_backward(*arg_s, o_s, lse_s, grad_o_s, False)
+    gq, gk, gv, gk1, gv1 = attend_backward(*arg_s, of_s, lse_s, grad_o_s, False)
     gkv1 = to_core(jnp.concatenate([gk1, gv1], axis=1))
     grad_kv = (jnp.concatenate([gk, gv], axis=1) + gkv1.astype(F32)).astype(BF)
     grad_qkv_s = jnp.concatenate([gq, grad_kv], axis=1)
     gw_qkv_e = dot_outer(xs, grad_qkv_s)
     grad_xs = grad_s1 + dot_back(grad_qkv_s, wqkv_e)
 
-    def home(source, target):
-        parts = [source[:span], source[span:], target[:span], target[span:]]
-        sent = pick(parts, depth)
-        back = [
-            swap(
-                sent[k],
-                lambda c, g, z: ((z ^ k) >> 1, g, block_of(c, (z ^ k) & 1)),
-            )
-            for k in range(4)
-        ]
-        return jnp.stack(pick(back, seat))
-
-    outputs = home(memory, decoded)
-    grads = home(grad_xs.astype(BF), grad_xt.astype(BF)).astype(F32)
-
-    def fold(value):
-        return value.reshape(-1, width, value.shape[1])
-
-    def pack(parts):
-        return jnp.concatenate([p.astype(BF) for p in parts], axis=1)
-
-    def down_columns(value):
-        return [value[i * width : (i + 1) * width] for i in range(value.shape[0] // width)]
-
-    ffn_d = pack([gw_up_d] + down_columns(gw_down_d))
-    rest_d = pack([gw_cross_out, gw_cross_q, gw_out_d, gw_qkv_d])
-    ffn_e = pack([gw_cross_kv, gw_up_e] + down_columns(gw_down_e))
-    rest_e = pack([gw_out_e, gw_qkv_e])
-    ffn_d, rest_d, ffn_e, rest_e = (
-        sum_over_all(v, core, group, depth, None) for v in (ffn_d, rest_d, ffn_e, rest_e)
-    )
-    kv_at = cross_kv_weight.shape[1]
-    shared_part = join_cores(
-        jnp.concatenate([rest_d[:, : 2 * width], ffn_e[:, :kv_at]], axis=1), core, None
-    )
-    mine = jnp.where(
-        core == 0,
-        jnp.concatenate([ffn_e[:, kv_at:], rest_e], axis=1),
-        jnp.concatenate([ffn_d, rest_d[:, 2 * width :]], axis=1),
-    )
-    theirs = jnp.where(
-        core == 0,
-        jnp.concatenate([ffn_d, rest_d[:, 2 * width :]], axis=1),
-        jnp.concatenate([ffn_e[:, kv_at:], rest_e], axis=1),
-    )
-    lacking = to_core(theirs)
-    whole = jnp.where(
-        core == 0,
-        jnp.concatenate([mine, lacking], axis=0),
-        jnp.concatenate([lacking, mine], axis=0),
-    ).astype(F32)
-    shared_part = shared_part.astype(F32)
-    ff = up_weight.shape[2]
-    g_up = whole[:, :ff]
-    g_down = jnp.concatenate(
-        [whole[:, ff + i * width : ff + (i + 1) * width] for i in range(ff // width)], axis=0
-    )
-    g_out = whole[:, 2 * ff : 2 * ff + width]
-    g_qkv = whole[:, 2 * ff + width :]
-    g_cross_out = shared_part[:, :width]
-    g_cross_q = shared_part[:, width : 2 * width]
-    g_cross_kv = shared_part[:, 2 * width :]
-
     small = jnp.stack(
         [gg_e0, gg_e1, gb_e0, gb_e1, gg_d0, gg_d1, gb_d0, gb_d1, gg_c, gb_c]
         + [jnp.zeros_like(gg_c)] * 6
     )
-    for move in (
-        to_core,
-        functools.partial(swap, move=lambda c, g, z: (c, g ^ 1, z)),
-        functools.partial(swap, move=lambda c, g, z: (c, g ^ 2, z)),
-        functools.partial(swap, move=lambda c, g, z: (c, g, z ^ 1)),
-        functools.partial(swap, move=lambda c, g, z: (c, g, z ^ 2)),
-    ):
-        small = small + move(small)
+    parts = (
+        gw_up_d, gw_down_d, gw_up_e, gw_down_e, gw_out_d, gw_qkv_d,
+        gw_out_e, gw_qkv_e, gw_cross_out, gw_cross_q, gw_cross_kv,
+    )
+    outputs, grads, sums, small = collect(
+        (memory, decoded),
+        (grad_xs.astype(BF), grad_xt.astype(BF)),
+        tuple(p.astype(BF) for p in parts),
+        small,
+    )
+    g_up, g_down, g_out, g_qkv, g_cross_out, g_cross_q, g_cross_kv = (
+        value.astype(F32) for value in sums
+    )
     layer_small = jnp.where(core == 0, small[:4], small[4:8])
     return (
         outputs[None],
-        grads[None],
+        grads.astype(F32)[None],
         g_qkv[None],
         g_out[None],
         g_up[None],

time: 483 us -> 381 us (0.79)
  Pallas kernels: 66.5 us -> 259 us
  waiting for transfers between devices: 143 us -> 0.02 us
  starting transfers between devices: 103 us -> 10.1 us
  other arithmetic: 54.8 us -> 30.2 us
  matrix products: 74 us -> 54.9 us
  local copies, waits for them, and re-layouts: 32.4 us -> 20.9 us
    pallas_call x0 -> x2, Pallas kernels: none -> 190 us  [the longest x1 161 us: collect(): pl.pallas_call(functools.partial(collect_kernel, groups), in_specs=[resid...]
    ppermute x69 -> x8, waiting for transfers between devices: 143 us -> 0.02 us  [swap(): return lax.ppermute(value, AXES, pairs)]
    ppermute x69 -> x8, starting transfers between devices: 103 us -> 10.1 us  [swap(): return lax.ppermute(value, AXES, pairs)]
    select_n x22 -> x0, other arithmetic: 16.1 us -> none  [the longest x16 10.5 us: sum_over_all(): jnp.where(bit == 0, jnp.concatenate([value, arrived], axis=0), jnp.concat...]
    convert_element_type x23 -> x3, other arithmetic: 19.6 us -> 4.9 us  [row_shards(): value.astype(F32)]
    dot_general x11, matrix products: 30.9 us -> 17.2 us  [dot_back(): lax.dot_general(a, b, (((1,), (1,)), ((), ())), preferred_element_type=F32)]
    dot_general x11, matrix products: 26.5 us -> 14.3 us  [dot(): lax.dot_general(a, b, (((1,), (0,)), ((), ())), preferred_element_type=F32)]
    broadcast_in_dim x1 -> x4, other arithmetic: 1.1 us -> 8.36 us  [the longest x1 2.54 us: row_shards(): g_up[None]]
  transfers between devices with their start and end apart: 69 -> 8, of which waited for: 32 -> 0; matrix products, arithmetic and copies ran while one was open for 23% -> 11% of each run, Pallas kernels for 9% -> 16%
where the time goes in v2:
time: 381 us; the launch traced here: 377 us
  Pallas kernels  259 us (68%)
  matrix products  54.9 us (14%)
  other arithmetic  30.2 us (8%)
  local copies, waits for them, and re-layouts  20.9 us (5%)
  starting transfers between devices  10.1 us (3%)
    pallas_call x1, Pallas kernels, collect(): pl.pallas_call(functools.partial(collect_kernel, groups), in_specs=[resid...  161 us
    pallas_call x3, Pallas kernels, attend_backward(): pl.pallas_call(functools.partial(attend_back_kernel, causal), grid=(steps...  40.9 us
    pallas_call x1, Pallas kernels, spread(): pl.pallas_call(functools.partial(spread_kernel, count), in_specs=[anywher...  29.2 us
    pallas_call x3, Pallas kernels, attend_forward(): pl.pallas_call(functools.partial(attend_kernel, causal), grid=(steps,), i...  27.6 us
    dot_general x11, matrix products, dot_outer(): lax.dot_general(a, b, (((0,), (0,)), ((), ())), preferred_element_type=F32)  23.4 us
    dot_general x11, matrix products, dot_back(): lax.dot_general(a, b, (((1,), (1,)), ((), ())), preferred_element_type=F32)  17.2 us
    dot_general x11, matrix products, dot(): lax.dot_general(a, b, (((1,), (0,)), ((), ())), preferred_element_type=F32)  14.3 us
    ppermute x8, starting transfers between devices, swap(): return lax.ppermute(value, AXES, pairs)  10.1 us
  transfers between devices with their start and end apart: 8, of which 0 were waited for; matrix products, arithmetic and copies ran while one was open for 11% of the time, Pallas kernels for 16%

profile of v2, /device:TPU:1, one launch (start us, length us, event | category | flops | bytes accessed | tf_op | source)
XLA Modules:
  0.0 377.0 jit_solution(5427521542918139395)
XLA Ops:
  0.7 1.9 dynamic-slice_bitcast_fusion.1
  2.5 6.6 %collective-permute-start.3 = (bf16[256,512]{1,0:T(8,128)(2,1)}, bf16[256,512]{1,0:T(8,128)(2,1)}, u32[]{:S(2)}, u32[]{:S(2)}) collective-permute-start(bf16[256,512]{1,0:T(8,128)(2,1)} %get-tuple-element.121), channel_id=1, source_target_pairs={{0,1},{1,17},{2,16},{3,0},{4,5},{5,21},{6,20},{7,4},{8,9},{9,25},{... | collective-permute-start | bytes 786440 | tf_op jit(solution)/shard_map/ppermute | solution.py:432
  9.1 1.9 collective-permute-start.4
  11.1 29.2 %spread.1 = (bf16[2,512,512]{2,1,0:T(8,128)(2,1)}, bf16[2,512,1536]{2,1,0:T(8,128)(2,1)}, bf16[2,512,512]{2,1,0:T(8,128)(2,1)}, bf16[2,512,2048]{2,1,0:T(8,128)(...) custom-call(bf16[4,256,512]{2,1,0:T(8,128)(2,1)} %bitcast.171, ...), custom_call_target="tpu_custom_call" | custom-call | tf_op jit(solution)/shard_map/spread/pallas_call | solution.py:785
  40.3 2.7 convolution_convert_fusion.2.q_ref.k_ref.v_ref
  53.7 9.7 %attend_forward.3 = (bf16[512,512]{1,0:T(8,128)(2,1)S(1)}, f32[512,512]{1,0:T(8,128)S(1)}, f32[512,512]{1,0:T(8,128)S(1)}) custom-call(bf16[512,1536]{1,0:T(8,128)(2,1)S(1)} %convolution_convert_fusion.3.q_ref.k_ref.v_ref, bf16[512,1536]{1,0:T(8,128)(2,1)S(1)} %convolution_convert_fusion.3.q_ref.k_ref.v_ref, ...), custom_call_target="tpu_custom_call" | custom-call | flops 2147483648 | bytes 4194304 | tf_op jit(solution)/shard_map/attend_forward/pallas_call | solution.py:624
  64.2 3.2 fusion.31
  71.5 8.8 %attend_forward.4 = (bf16[512,512]{1,0:T(8,128)(2,1)S(1)}, f32[512,512]{1,0:T(8,128)S(1)}, f32[512,512]{1,0:T(8,128)S(1)}) custom-call(bf16[512,1536]{1,0:T(8,128)(2,1)S(1)} %copy-done.6, bf16[512,1536]{1,0:T(8,128)(2,1)S(1)} %copy-done.6, bf16[512,1536]{1,0:T(8,128)(2,1)S(1)} %copy-done.6, bf16[512,1024]{1,0:T(8,128)(2,1)} %collective-permute-done.1.ko_ref.vo_ref, ...), custom_call_target="tpu_custom_call" | custom-call | flops 2147483648 | bytes 4194304 | tf_op jit(solution)/shard_map/attend_forward/pallas_call | solution.py:624
  82.3 9.1 %attend_forward.5 = (bf16[512,512]{1,0:T(8,128)(2,1)S(1)}, f32[512,512]{1,0:T(8,128)S(1)}, f32[512,512]{1,0:T(8,128)S(1)}) custom-call(bf16[512,512]{1,0:T(8,128)(2,1)S(1)} %convolution_convert_fusion.17.q_ref, bf16[512,1024]{1,0:T(8,128)(2,1)S(1)} %convolution_convert_fusion.9.k_ref.v_ref, bf16[512,1024]{1,0:T(8,128)(2,1)S(1)} %convolution_convert_fusion.9.k_ref.v_ref, ...), custom_call_target="tpu_custom_call" | custom-call | flops 2147483648 | bytes 4194304 | tf_op jit(solution)/shard_map/attend_forward/pallas_call | solution.py:624
  92.4 2.1 copy-done.47
  100.4 3.5 fusion.13
  107.8 14.6 %attend_backward.3 = (bf16[512,512]{1,0:T(8,128)(2,1)S(1)}, f32[512,512]{1,0:T(8,128)S(1)}, f32[512,512]{1,0:T(8,128)S(1)}, bf16[512,512]{1,0:T(8,128)(2,1)S(1)}, bf16[512,512]{1,0:T(8,128)(2,1)S(1)}) custom-call(bf16[512,512]{1,0:T(8,128)(2,1)S(1)} %convolution_convert_fusion.17.q_ref, bf16[512,1024]{1,0:T(8,128)(2,1)S(1)} %convolution_convert_fusion.9.k_ref.v_ref, ...), custom_call_target="tpu_custom_call" | custom-call | flops 5368709120 | bytes 7864320 | tf_op jit(solution)/shard_map/attend_backward/pallas_call | solution.py:646
  125.4 2.8 convolution_convert_fusion.7.refs_4_
  128.2 3.2 convolution_convert_fusion.6.refs_5_
  135.6 3.5 fusion.6
  140.8 2.7 convolution_convert_fusion.5.refs_6_
  145.3 12.1 %attend_backward.5 = (bf16[512,512]{1,0:T(8,128)(2,1)S(1)}, f32[512,512]{1,0:T(8,128)S(1)}, f32[512,512]{1,0:T(8,128)S(1)}, bf16[512,512]{1,0:T(8,128)(2,1)S(1)}, bf16[512,512]{1,0:T(8,128)(2,1)S(1)}) custom-call(bf16[512,1536]{1,0:T(8,128)(2,1)} %copy-done.5, bf16[512,1536]{1,0:T(8,128)(2,1)} %copy-done.5, bf16[512,1536]{1,0:T(8,128)(2,1)} %copy-done.5, ...), custom_call_target="tpu_custom_call" | custom-call | flops 5368709120 | bytes 7864320 | tf_op jit(solution)/shard_map/attend_backward/pallas_call | solution.py:646
  159.1 14.2 %attend_backward.4 = (bf16[512,512]{1,0:T(8,128)(2,1)S(1)}, f32[512,512]{1,0:T(8,128)S(1)}, f32[512,512]{1,0:T(8,128)S(1)}, bf16[512,512]{1,0:T(8,128)(2,1)S(1)}, bf16[512,512]{1,0:T(8,128)(2,1)S(1)}) custom-call(bf16[512,1536]{1,0:T(8,128)(2,1)} %copy-done.4, bf16[512,1536]{1,0:T(8,128)(2,1)} %copy-done.4, bf16[512,1536]{1,0:T(8,128)(2,1)} %copy-done.4, ...), custom_call_target="tpu_custom_call" | custom-call | flops 5368709120 | bytes 7864320 | tf_op jit(solution)/shard_map/attend_backward/pallas_call | solution.py:646
  175.0 1.7 convolution_convert_fusion.8.refs_14_
  178.0 3.2 convolution_convert_fusion.4.refs_7_
  183.8 1.7 fusion.16
  185.5 2.1 convolution_convert_fusion.1.refs_9_
  188.2 1.8 fusion.73.refs_3_
  190.0 1.7 fusion.15
  191.8 1.8 fusion.76.refs_2_
  193.6 2.2 convolution_convert_fusion.refs_11_
  195.7 161.3 %collect.1 = (bf16[4,256,512]{2,1,0:T(8,128)(2,1)}, bf16[4,256,512]{2,1,0:T(8,128)(2,1)}, bf16[512,2048]{1,0:T(8,128)(2,1)}, bf16[2048,512]{1,0:T(8,128)(2,1)}, ...) custom-call(bf16[512,512]{1,0:T(8,128)(2,1)} %copy-done.30, ...), custom_call_target="tpu_custom_call" | custom-call | tf_op jit(solution)/shard_map/collect/pallas_call | solution.py:1089
  359.9 2.1 bitcast_convert_fusion.4
  362.0 2.2 convert_element_type.218
  368.5 2.1 bitcast_convert_fusion.2
  370.6 2.5 bitcast_convert_fusion.1
  373.2 2.6 bitcast_convert_fusion
  (237 shorter events, 54.2 us)
Async XLA Ops:
  0.6 70.0 %copy-start = (bf16[512,1024]{1,0:T(8,128)(2,1)S(1)}, bf16[512,1024]{1,0:T(8,128)(2,1)}, u32[]{:S(2)}) copy-start(bf16[512,1024]{1,0:T(8,128)(2,1)} %param.28) | copy-start | bytes 3145732
  2.5 50.0 %collective-permute-start.3 = (bf16[256,512]{1,0:T(8,128)(2,1)}, bf16[256,512]{1,0:T(8,128)(2,1)}, u32[]{:S(2)}, u32[]{:S(2)}) collective-permute-start(bf16[256,512]{1,0:T(8,128)(2,1)} %get-tuple-element.121), channel_id=1, source_target_pairs={{0,1},{1,17},{2,16},{3,0},{4,5},{5,21},{6,20},{7,4},{8,9},{9,25},{... | collective-permute-start | bytes 786440 | tf_op jit(solution)/shard_map/ppermute | solution.py:432
  9.1 43.4 %collective-permute-start.4 = (bf16[256,512]{1,0:T(8,128)(2,1)S(1)}, bf16[256,512]{1,0:T(8,128)(2,1)}, u32[]{:S(2)}, u32[]{:S(2)}) collective-permute-start(bf16[256,512]{1,0:T(8,128)(2,1)S(1)} %get-tuple-element.122), channel_id=1, source_target_pairs={{0,0},{1,16},{2,17},{3,1},{4,4},{5,20},{6,21},{7,5},{8,8},{9,24},{... | collective-permute-start | bytes 786440 | tf_op jit(solution)/shard_map/ppermute | solution.py:432
  40.3 4.0 %copy-start.38 = (bf16[2,512,512]{2,1,0:T(8,128)(2,1)S(1)}, bf16[2,512,512]{2,1,0:T(8,128)(2,1)}, u32[]{:S(2)}) copy-start(bf16[2,512,512]{2,1,0:T(8,128)(2,1)} %get-tuple-element.54) | copy-start | bytes 3145732
  44.3 6.7 %copy-start.44 = (f32[2,2,512]{2,1,0:T(2,128)S(1)}, f32[2,2,512]{2,1,0:T(2,128)}, u32[]{:S(2)}) copy-start(f32[2,2,512]{2,1,0:T(2,128)} %get-tuple-element.58) | copy-start | bytes 24580
  44.3 6.7 %copy-start.43 = (f32[2,2,512]{2,1,0:T(2,128)S(1)}, f32[2,2,512]{2,1,0:T(2,128)}, u32[]{:S(2)}) copy-start(f32[2,2,512]{2,1,0:T(2,128)} %get-tuple-element.59) | copy-start | bytes 24580
  44.3 27.2 %collective-permute-start.1 = (bf16[512,1024]{1,0:T(8,128)(2,1)}, bf16[512,1024]{1,0:T(8,128)(2,1)}, u32[]{:S(2)}, u32[]{:S(2)}) collective-permute-start(bf16[512,1024]{1,0:T(8,128)(2,1)} %slice.136), channel_id=1, source_target_pairs={{0,16},{1,17},{2,18},{3,19},{4,20},{5,21},{6,22},{7,23},{8,24},{9,... | collective-permute-start | bytes 3145736 | tf_op jit(solution)/shard_map/ppermute | solution.py:432
  45.3 18.1 %copy-start.4 = (bf16[512,1536]{1,0:T(8,128)(2,1)}, bf16[512,1536]{1,0:T(8,128)(2,1)S(1)}, u32[]{:S(2)}) copy-start(bf16[512,1536]{1,0:T(8,128)(2,1)S(1)} %convolution_convert_fusion.3.q_ref.k_ref.v_ref) | copy-start | bytes 4718596
  46.6 7.1 %collective-permute-start = (bf16[512,1024]{1,0:T(8,128)(2,1)}, bf16[512,1024]{1,0:T(8,128)(2,1)}, u32[]{:S(2)}, u32[]{:S(2)}) collective-permute-start(bf16[512,1024]{1,0:T(8,128)(2,1)} %slice.135), channel_id=1, source_target_pairs={{0,16},{1,17},{2,18},{3,19},{4,20},{5,21},{6,22},{7,23},{8,24},{9,... | collective-permute-start | bytes 3145736 | tf_op jit(solution)/shard_map/ppermute | solution.py:432
  53.7 9.7 %copy-start.26 = (bf16[2,512,512]{2,1,0:T(8,128)(2,1)S(1)}, bf16[2,512,512]{2,1,0:T(8,128)(2,1)}, u32[]{:S(2)}) copy-start(bf16[2,512,512]{2,1,0:T(8,128)(2,1)} %get-tuple-element.57) | copy-start | bytes 3145732
  53.7 9.7 %copy-start.39 = (bf16[2,512,512]{2,1,0:T(8,128)(2,1)S(1)}, bf16[2,512,512]{2,1,0:T(8,128)(2,1)}, u32[]{:S(2)}) copy-start(bf16[2,512,512]{2,1,0:T(8,128)(2,1)} %get-tuple-element.54) | copy-start | bytes 3145732
  63.4 4.1 %copy-start.8 = (f32[512,512]{1,0:T(8,128)}, f32[512,512]{1,0:T(8,128)S(1)}, u32[]{:S(2)}) copy-start(f32[512,512]{1,0:T(8,128)S(1)} %get-tuple-element.70.o_ref) | copy-start | bytes 3145732
  63.4 4.1 %copy-start.9 = (f32[512,512]{1,0:T(8,128)}, f32[512,512]{1,0:T(8,128)S(1)}, u32[]{:S(2)}) copy-start(f32[512,512]{1,0:T(8,128)S(1)} %get-tuple-element.71.lse_ref) | copy-start | bytes 3145732
  70.7 104.3 %copy-start.30 = (bf16[512,512]{1,0:T(8,128)(2,1)}, bf16[512,512]{1,0:T(8,128)(2,1)S(1)}, u32[]{:S(2)}) copy-start(bf16[512,512]{1,0:T(8,128)(2,1)S(1)} %add_convert_fusion.1.refs_0_) | copy-start | bytes 1572868
  71.4 10.8 %collective-permute-start.2 = (bf16[512,1024]{1,0:T(8,128)(2,1)S(1)}, bf16[512,1024]{1,0:T(8,128)(2,1)S(1)}, u32[]{:S(2)}, u32[]{:S(2)}) collective-permute-start(bf16[512,1024]{1,0:T(8,128)(2,1)S(1)} %convolution_convert_fusion.9.k_ref.v_ref), channel_id=1, source_target_pairs={{0,16},{1,17},{2,18},{3,19},{4,20},{5,21},{6,22},{7,23},{8,24},{9,... | collective-permute-start | bytes 3145736 | tf_op jit(solution)/shard_map/ppermute | solution.py:432
  80.3 11.1 %copy-start.10 = (f32[512,512]{1,0:T(8,128)}, f32[512,512]{1,0:T(8,128)S(1)}, u32[]{:S(2)}) copy-start(f32[512,512]{1,0:T(8,128)S(1)} %get-tuple-element.78.o_ref) | copy-start | bytes 3145732
  80.3 11.1 %copy-start.11 = (f32[512,512]{1,0:T(8,128)}, f32[512,512]{1,0:T(8,128)S(1)}, u32[]{:S(2)}) copy-start(f32[512,512]{1,0:T(8,128)S(1)} %get-tuple-element.79.lse_ref) | copy-start | bytes 3145732
  82.3 9.2 %copy-start.31 = (bf16[512,512]{1,0:T(8,128)(2,1)S(1)}, bf16[512,512]{1,0:T(8,128)(2,1)}, u32[]{:S(2)}) copy-start(bf16[512,512]{1,0:T(8,128)(2,1)} %param.29) | copy-start | bytes 1572868
  82.3 9.2 %copy-start.7 = (bf16[512,1024]{1,0:T(8,128)(2,1)}, bf16[512,1024]{1,0:T(8,128)(2,1)S(1)}, u32[]{:S(2)}) copy-start(bf16[512,1024]{1,0:T(8,128)(2,1)S(1)} %collective-permute-done.2.ko_ref.vo_ref) | copy-start | bytes 3145732
  91.4 4.3 %copy-start.12 = (f32[512,512]{1,0:T(8,128)}, f32[512,512]{1,0:T(8,128)S(1)}, u32[]{:S(2)}) copy-start(f32[512,512]{1,0:T(8,128)S(1)} %get-tuple-element.64.o_ref) | copy-start | bytes 3145732
  91.5 4.3 %copy-start.13 = (f32[512,512]{1,0:T(8,128)}, f32[512,512]{1,0:T(8,128)S(1)}, u32[]{:S(2)}) copy-start(f32[512,512]{1,0:T(8,128)S(1)} %get-tuple-element.65.lse_ref) | copy-start | bytes 3145732
  124.9 6.5 %collective-permute-start.5 = (bf16[512,1024]{1,0:T(8,128)(2,1)S(1)}, bf16[512,1024]{1,0:T(8,128)(2,1)S(1)}, u32[]{:S(2)}, u32[]{:S(2)}) collective-permute-start(bf16[512,1024]{1,0:T(8,128)(2,1)S(1)} %pad_maximum_fusion.2), channel_id=1, source_target_pairs={{0,16},{1,17},{2,18},{3,19},{4,20},{5,21},{6,22},{7,23},{8,24},{9,... | collective-permute-start | bytes 3145736 | tf_op jit(solution)/shard_map/ppermute | solution.py:432
  131.4 4.2 %copy-start.58 = (f32[512,2048]{1,0:T(8,128)S(1)}, f32[512,2048]{1,0:T(8,128)}, u32[]{:S(2)}) copy-start(f32[512,2048]{1,0:T(8,128)} %copy-done.57) | copy-start | bytes 12582916
  132.9 6.2 %copy-start.35 = (f32[512,512]{1,0:T(8,128)}, f32[512,512]{1,0:T(8,128)S(1)}, u32[]{:S(2)}) copy-start(f32[512,512]{1,0:T(8,128)S(1)} %get-tuple-element.115) | copy-start | bytes 3145732
  144.3 32.4 %copy-start.22 = (f32[512,512]{1,0:T(8,128)}, f32[512,512]{1,0:T(8,128)S(1)}, u32[]{:S(2)}) copy-start(f32[512,512]{1,0:T(8,128)S(1)} %get-tuple-element.111) | copy-start | bytes 3145732
  144.3 37.0 %copy-start.20 = (f32[512,512]{1,0:T(8,128)}, f32[512,512]{1,0:T(8,128)S(1)}, u32[]{:S(2)}) copy-start(f32[512,512]{1,0:T(8,128)S(1)} %get-tuple-element.162) | copy-start | bytes 3145732
  158.5 25.3 %collective-permute-start.7 = (bf16[512,1024]{1,0:T(8,128)(2,1)}, bf16[512,1024]{1,0:T(8,128)(2,1)}, u32[]{:S(2)}, u32[]{:S(2)}) collective-permute-start(bf16[512,1024]{1,0:T(8,128)(2,1)} %pad_maximum_fusion.4), channel_id=1, source_target_pairs={{0,16},{1,17},{2,18},{3,19},{4,20},{5,21},{6,22},{7,23},{8,24},{9,... | collective-permute-start | bytes 3145736 | tf_op jit(solution)/shard_map/ppermute | solution.py:432
  159.1 15.9 %copy-start.55 = (bf16[512,1024]{1,0:T(8,128)(2,1)S(1)}, bf16[512,1024]{1,0:T(8,128)(2,1)}, u32[]{:S(2)}) copy-start(bf16[512,1024]{1,0:T(8,128)(2,1)} %copy-done.54) | copy-start | bytes 3145732
  174.5 15.5 %collective-permute-start.6 = (bf16[512,1024]{1,0:T(8,128)(2,1)}, bf16[512,1024]{1,0:T(8,128)(2,1)}, u32[]{:S(2)}, u32[]{:S(2)}) collective-permute-start(bf16[512,1024]{1,0:T(8,128)(2,1)} %pad_maximum_fusion.3), channel_id=1, source_target_pairs={{0,16},{1,17},{2,18},{3,19},{4,20},{5,21},{6,22},{7,23},{8,24},{9,... | collective-permute-start | bytes 3145736 | tf_op jit(solution)/shard_map/ppermute | solution.py:432
  357.0 7.2 %copy-start.42 = (bf16[512,512]{1,0:T(8,128)(2,1)S(1)}, bf16[512,512]{1,0:T(8,128)(2,1)}, u32[]{:S(2)}) copy-start(bf16[512,512]{1,0:T(8,128)(2,1)} %get-tuple-element.94) | copy-start | bytes 1572868
  357.0 8.3 %copy-start.34 = (bf16[4,256,512]{2,1,0:T(8,128)(2,1)S(1)}, bf16[4,256,512]{2,1,0:T(8,128)(2,1)}, u32[]{:S(2)}) copy-start(bf16[4,256,512]{2,1,0:T(8,128)(2,1)} %get-tuple-element.86) | copy-start | bytes 3145732
  362.0 5.0 %copy-start.33 = (bf16[512,1024]{1,0:T(8,128)(2,1)S(1)}, bf16[512,1024]{1,0:T(8,128)(2,1)}, u32[]{:S(2)}) copy-start(bf16[512,1024]{1,0:T(8,128)(2,1)} %get-tuple-element.93) | copy-start | bytes 3145732
  (40 other events, 100.4 us)
